TPU v7x, 32 devices: a whole 2x2x4 slice. The times are simulated.
32 devices in a mesh: groups: 2 (over y), space: 16 (over z, x, core).
Axes of the slice: x: 2, y: 2, z: 4, core: 2. Of those that a mesh axis runs over, the one named last changes fastest.
Arguments:
- block_features: bfloat16 [64, 64, 4096], P(('groups', 'space')), parts along dimension 0
- cotangent: bfloat16 [64, 64, 4096], P(('groups', 'space')), parts along dimension 0
- coords: int32 [64, 3], P('groups'), parts along dimension 0, may hold values from -1 to 255, as said below
- conv1_weight: bfloat16 [64, 1728], replicated, may hold values from -0.15625 to 0.15625
- conv1_bias: float32 [64], replicated, may hold values from -1 to 1
- conv2_weight: bfloat16 [64, 1728], replicated, may hold values from -0.15625 to 0.15625
Outputs:
- grad_features: bfloat16 [64, 64, 4096], P(('groups', 'space')), parts along dimension 0
- grad_conv1_weight: float32 [128, 1728], P('groups'), parts along dimension 0
- grad_conv2_weight: float32 [128, 1728], P('groups'), parts along dimension 0
- grad_conv1_bias: float32 [128], P('groups'), parts along dimension 0
There are 2 independent parts, one for each index of `groups`. A program takes and returns all parts, laid end to end along the dimension named above; an argument that names none is the same for every part. Nothing has to cross between parts.
Inputs may be any that keep to these rules, and one draw needn't show every extreme that they name: `coords`: the rows of slab i are slots i * 2 to i * 2 + 1; an active slot of slab i has first coordinate i; empty slots hold -1 in all three coordinates; the active slots of a slab come before its empty ones; no two active slots share coordinates; slabs i and i + 8 hold at most 2 active blocks together.
All inputs are finite; a program needn't handle non-finite values.
Results may differ from a plain program's by a relative error of at most 0.0055.
Values may be sent and summed in bfloat16 or wider, within the bound.
A program may use at most 128 MiB of HBM per device.

v0:
```python
import jax
import jax.numpy as jnp
import numpy as np
from jax import lax
from jax.sharding import PartitionSpec as P

CH = 64
BLOCK = 16


neighbour_steps = (
    np.stack(np.meshgrid(np.arange(-1, 2), np.arange(-1, 2), np.arange(-1, 2), indexing="ij"), -1)
    .reshape(27, 3)
    .astype(np.int32)
)
clip_norm = 256.0


def padded(block, sides, width):
    for axis, dim in sides:
        count = lax.axis_size(axis)
        forward = [(i, i + 1) for i in range(count - 1)]
        backward = [(target, source) for source, target in forward]
        low = lax.ppermute(
            lax.slice_in_dim(block, block.shape[dim] - width, None, axis=dim), axis, forward
        )
        high = lax.ppermute(lax.slice_in_dim(block, 0, width, axis=dim), axis, backward)
        block = jnp.concatenate([low, block, high], axis=dim)
    return block


def trimmed(region, offset_step, axis_number, block_edge):
    if offset_step < 0:
        return lax.slice_in_dim(region, block_edge - 2, block_edge, axis=axis_number)
    if offset_step > 0:
        return lax.slice_in_dim(region, 0, 2, axis=axis_number)
    return region


def conv_valid(inputs, kernel):
    return lax.conv_general_dilated(
        inputs,
        kernel,
        (1, 1, 1),
        "VALID",
        dimension_numbers=("NCDHW", "OIDHW", "NCDHW"),
        preferred_element_type=jnp.float32,
    )


def flipped(kernel):
    return jnp.transpose(kernel[:, :, ::-1, ::-1, ::-1], (1, 0, 2, 3, 4))


def filter_sums(source, target):
    edge = target.shape[-1]
    out_channels = target.shape[0]
    in_channels = source.shape[0]
    flat_target = target.reshape(out_channels, -1)
    products = []
    for x_step in range(3):
        for y_step in range(3):
            for z_step in range(3):
                window = source[
                    :, x_step : x_step + edge, y_step : y_step + edge, z_step : z_step + edge
                ].reshape(in_channels, -1)
                products.append(
                    jnp.einsum("ou,iu->oi", flat_target, window, preferred_element_type=jnp.float32)
                )
    return jnp.stack(products, axis=2).reshape(out_channels, -1)


def live_region(cell_flags, block_edge):
    position = jnp.arange(block_edge + 2)
    sub_part = (position >= 1).astype(jnp.int32) + (position >= block_edge + 1).astype(jnp.int32)
    selector = (sub_part[:, None] == jnp.arange(3)[None, :]).astype(jnp.float32)
    return jnp.einsum("ai,bj,ck,ijk->abc", selector, selector, selector, cell_flags)


def block_grads(padded_tile, cell_flags, conv1_weight, conv1_bias, conv2_weight):
    block_edge = padded_tile.shape[-1] - 4
    channels = conv1_weight.shape[0]
    first_kernel = conv1_weight.reshape(channels, channels, 3, 3, 3)
    second_kernel = conv2_weight.reshape(channels, channels, 3, 3, 3)
    features = padded_tile[0]
    upstream = padded_tile[1]
    live_mask = live_region(cell_flags, block_edge)
    pre_act = conv_valid(features[None], first_kernel)[0] + conv1_bias[:, None, None, None]
    sigmoid_pre = 1.0 / (1.0 + jnp.exp(-pre_act))
    hidden = (pre_act * sigmoid_pre * live_mask).astype(jnp.bfloat16)
    back_hidden = conv_valid(upstream[None], flipped(second_kernel))[0]
    grad_pre = (
        back_hidden * sigmoid_pre * (1.0 + pre_act * (1.0 - sigmoid_pre)) * live_mask
    ).astype(jnp.bfloat16)
    inner_grad = grad_pre[:, 1 : block_edge + 1, 1 : block_edge + 1, 1 : block_edge + 1]
    own_upstream = upstream[:, 2 : block_edge + 2, 2 : block_edge + 2, 2 : block_edge + 2]
    spread_back = conv_valid(grad_pre[None], flipped(first_kernel))[0]
    grad_out = (
        (own_upstream.astype(jnp.float32) + spread_back).astype(jnp.bfloat16).reshape(channels, -1)
    )
    grad_first = filter_sums(
        features[:, 1 : block_edge + 3, 1 : block_edge + 3, 1 : block_edge + 3], inner_grad
    )
    grad_second = filter_sums(hidden, own_upstream)
    grad_bias = jnp.sum(inner_grad.astype(jnp.float32), axis=(1, 2, 3))
    return (grad_out, grad_first, grad_second, grad_bias)


def slot_matches(padded_coords, slab_index, slot_index):
    nearby = lax.dynamic_slice_in_dim(padded_coords, slab_index * 2, 6, 0)
    own_row = nearby[2 + slot_index]
    targets = own_row[None, :] + jnp.asarray(neighbour_steps)
    grouped = jnp.repeat(nearby.reshape(3, 2, 3), 9, axis=0)
    return jnp.all(grouped == targets[:, None, :], axis=2) & (grouped[:, :, 0] >= 0)


def flags_from(matched):
    return (matched[:, 0] | matched[:, 1]).astype(jnp.float32).reshape(3, 3, 3)


def build_tile(sources, matched, block_edge):
    planes = []
    for x_step in range(3):
        source = sources[x_step]
        row_list = []
        for y_step in range(3):
            line_parts = []
            for z_step in range(3):
                offset_index = x_step * 9 + y_step * 3 + z_step
                first_region = trimmed(
                    trimmed(source[0], y_step - 1, 3, block_edge), z_step - 1, 4, block_edge
                )
                second_region = trimmed(
                    trimmed(source[1], y_step - 1, 3, block_edge), z_step - 1, 4, block_edge
                )
                region = jnp.where(
                    matched[offset_index, 0],
                    first_region,
                    jnp.where(
                        matched[offset_index, 1], second_region, jnp.zeros_like(first_region)
                    ),
                )
                line_parts.append(region)
            row_list.append(jnp.concatenate(line_parts, axis=4))
        planes.append(jnp.concatenate(row_list, axis=3))
    return jnp.concatenate(planes, axis=2)


def body(block_features, cotangent, coords, conv1_weight, conv1_bias, conv2_weight):
    block_edge = BLOCK
    channels = CH
    slab_index = lax.axis_index("space")
    fields = jnp.stack([block_features, cotangent], axis=1).reshape(
        2, 2, channels, block_edge, block_edge * block_edge
    )
    face_layers = jnp.concatenate(
        [fields[:, :, :, 0:2], fields[:, :, :, block_edge - 2 : block_edge]], axis=3
    )
    received = padded(face_layers, (("space", 3),), 2)
    layer_shape = (2, 2, channels, 2, block_edge, block_edge)
    sources = (
        received[:, :, :, 0:2].reshape(layer_shape),
        fields.reshape(2, 2, channels, block_edge, block_edge, block_edge),
        received[:, :, :, 6:8].reshape(layer_shape),
    )
    padded_coords = jnp.pad(coords, ((2, 2), (0, 0)), constant_values=-1)
    own_rows = lax.dynamic_slice_in_dim(padded_coords, slab_index * 2 + 2, 2, 0)

    def compute_block(operand):
        return block_grads(operand[0], operand[1], conv1_weight, conv1_bias, conv2_weight)

    def empty_block(operand):
        return (
            jnp.zeros((channels, block_edge**3), jnp.bfloat16),
            jnp.zeros((channels, 27 * channels), jnp.float32),
            jnp.zeros((channels, 27 * channels), jnp.float32),
            jnp.zeros((channels,), jnp.float32),
        )

    outcome = []
    for slot_index in range(2):
        matched = slot_matches(padded_coords, slab_index, slot_index)
        operand = (build_tile(sources, matched, block_edge), flags_from(matched))
        outcome.append(lax.cond(own_rows[slot_index, 0] >= 0, compute_block, empty_block, operand))
    grad_features = jnp.stack([outcome[0][0], outcome[1][0]])
    grad_first = outcome[0][1] + outcome[1][1]
    grad_second = outcome[0][2] + outcome[1][2]
    grad_bias = outcome[0][3] + outcome[1][3]
    raw_first, raw_second, raw_bias = lax.psum((grad_first, grad_second, grad_bias), "space")
    norm_total = jnp.sqrt(
        jnp.sum(raw_first * raw_first)
        + jnp.sum(raw_second * raw_second)
        + jnp.sum(raw_bias * raw_bias)
    )
    clip_scale = jnp.minimum(1.0, clip_norm / (norm_total + 1e-06))
    return (grad_features, clip_scale * raw_first, clip_scale * raw_second, clip_scale * raw_bias)


def solution(mesh):
    placed = (
        P(("groups", "space"), None, None),
        P(("groups", "space"), None, None),
        P("groups", None),
        P(),
        P(),
        P(),
    )
    return jax.shard_map(
        body,
        mesh=mesh,
        in_specs=placed,
        out_specs=(
            P(("groups", "space"), None, None),
            P("groups", None),
            P("groups", None),
            P("groups"),
        ),
        check_vma=False,
    )
```

profile of v0, /device:TPU:0, one launch (start us, length us, event | category | flops | bytes accessed | tf_op | source)
XLA Modules:
  0.0 655.5 jit_solution(132371124198501241)
XLA Ops:
  7.2 2.1 copy.195
  9.3 1.8 copy.196
  11.2 2.2 pad_maximum_fusion.3
  13.4 3.2 collective-permute-start
  16.5 1.3 collective-permute-start.1
  25.4 2.7 fusion.402
  28.1 2.1 copy.67
  30.3 1.8 copy.68
  32.1 4.5 select_select_fusion.1
  36.6 5.1 broadcast_select_fusion.37
  41.8 5.2 broadcast_select_fusion.39
  46.9 6.2 broadcast_select_fusion.11
  53.1 5.1 select_select_fusion.8
  58.2 1.1 fusion.407
  59.3 5.1 broadcast_select_fusion.73
  64.4 4.9 select_select_fusion.17
  69.3 5.1 broadcast_select_fusion.75
  74.4 5.1 broadcast_select_fusion.43
  79.5 1.1 fusion.408
  80.6 5.1 broadcast_select_fusion.65
  85.7 5.0 broadcast_select_fusion.67
  90.8 5.1 broadcast_select_fusion.31
  95.9 5.0 select_select_fusion.15
  100.9 4.9 select_select_fusion.6
  105.9 43.3 %maximum_maximum_fusion = bf16[2,64,20,20,20]{1,4,3,2,0:T(8,128)(2,1)} fusion(bf16[2,64,2,2,2]{1,4,3,2,0:T(2,128)(2,1)S(1)} %get-tuple-element.158, bf16[2,64,2,2,16]{1,4,3,2,0:T(8,128)(2,1)S(1)} %get-tuple-element.155, bf16[2,64,2,2,2]{1,4,3,2,0:T(2,128)(2,1)S(1)} %get-tuple-element.159, bf16[2,64,2,16,2]{1,4,3,2,0:T(2,128)(2,1)S(1)} %get-tuple-element.163, ...), kind=kLoop, calls=%fused_computation.530 | loop fusion | flops 55296000 | bytes 4096000 | tf_op jit(solution)/shard_map/concatenate | solution.py:146
  149.1 43.3 %maximum_maximum_fusion.1 = bf16[2,64,20,20,20]{1,4,3,2,0:T(8,128)(2,1)} fusion(bf16[2,64,2,2,2]{1,4,3,2,0:T(2,128)(2,1)S(1)} %get-tuple-element.157, bf16[2,64,2,2,16]{1,4,3,2,0:T(8,128)(2,1)S(1)} %get-tuple-element.154, bf16[2,64,2,2,2]{1,4,3,2,0:T(2,128)(2,1)S(1)} %get-tuple-element.151, bf16[2,64,2,16,2]{1,4,3,2,0:T(2,128)(2,1)S(1)} %get-tuple-element.162, ...), kind=kLoop, calls=%fused_computation.531 | loop fusion | flops 55296000 | bytes 4096000 | tf_op jit(solution)/shard_map/concatenate | solution.py:146
  192.4 159.6 %conditional.2 = (f32[64]{0:T(128)}, bf16[1,64,4096]{2,1,0:T(8,128)(2,1)}, f32[64,1728]{1,0:T(8,128)}, f32[64,1728]{1,0:T(8,128)}) conditional(s32[]{:T(128)} %bitcast.418, () %tuple.28, (bf16[2,64,20,20,20]{1,4,3,2,0:T(8,128)(2,1)}, bf16[64,1728]{1,0:T(8,128)(2,1)S(1)}, bf16[64,1728]{1,0:T(8,128)(2,1)S(1)}, f32[64]{0:T(128)S(1)}, ...), branch_computations={%region_1.2_spmd, %region_2.4_spmd} | conditional | flops 6641546240 | bytes 250174368 | solution.py:184
  194.5 1.1 copy.35
  196.2 6.0 slice_bitcast_fusion.2
  206.2 15.3 %broadcast_select_fusion = f32[18,18,8,3,64]{4,2,3,1,0:T(8,128)S(1)} fusion(pred[8,3]{0,1:T(4,128)(4,1)S(1)} %copy-done.31, bf16[64,64,3,3,3]{1,0,4,3,2:T(8,128)(2,1)S(1)} %copy.35, bf16[64,20,20,1,7,2]{0,4,5,2,1,3:T(8,128)(2,1)S(1)} %slice.1345, bf16[64,20,20,1,8,3]{0,4,5,2,1,3:T(8,128)(2,1)S(1)} %copy.34), kind=kOutput, calls=%fused_computation.48 | convolution fusion | flops 1726568448 | bytes 4157464 | tf_op jit(solution)/shard_map/cond/branch_1_fun/conv_general_dilated | solution.py:41
  221.5 17.3 %add_multiply_fusion = (f32[18,18,8,3,64]{4,2,3,1,0:T(8,128)S(1)}, f32[18,18,8,3,64]{4,2,3,1,0:T(8,128)}) fusion(f32[18,18,8,3,64]{4,2,3,1,0:T(8,128)S(1)} %broadcast_select_fusion, f32[64]{0:T(128)S(1)} %get-tuple-element.25, bf16[64,64,3,3,3]{0,4,3,2,1:T(4,128)(2,1)S(1)} %reshape.143, bf16[64,20,20,1,7,2]{0,4,5,2,1,3:T(8,128)(2,1)S(1)} %slice.1343, ...), kind=kOutput, calls=%fused_computation.22 | convolution fusion | flops 1731047424 | bytes 8139032 | tf_op jit(solution)/shard_map/cond/branch_1_fun/conv_general_dilated | solution.py:41
  238.9 4.0 copy.39
  242.8 7.4 %reshape.170 = f32[18,18,1,24,64]{4,3,1,0,2:T(8,128)} reshape(f32[18,18,8,3,64]{4,3,2,1,0:T(4,128)} %copy.39) | data formatting | bytes 3981312 | tf_op jit(solution)/shard_map/cond/branch_1_fun/mul | solution.py:93
  250.2 2.8 fusion.34
  253.0 1.8 pad.9
  254.8 5.3 reshape.173
  261.1 6.3 fusion.39
  268.2 1.5 copy-done.5
  269.7 1.0 fusion.31
  270.7 1.1 copy.198
  271.9 6.1 copy.36
  278.0 7.4 %reshape.168 = f32[18,18,1,24,64]{4,3,1,0,2:T(8,128)} reshape(f32[18,18,8,3,64]{4,3,2,1,0:T(4,128)} %copy.36) | data formatting | bytes 3981312 | tf_op jit(solution)/shard_map/cond/branch_1_fun/conv_general_dilated | solution.py:41
  285.4 5.8 multiply_convert_fusion
  304.2 0.9 fusion.49
  309.0 1.9 copy.210
  311.0 1.9 reshape.417
  312.9 5.3 add_divide_fusion
  318.2 4.0 copy.31
  322.2 7.4 %reshape.161 = f32[18,18,1,24,64]{4,3,1,0,2:T(8,128)} reshape(f32[18,18,8,3,64]{4,3,2,1,0:T(4,128)} %copy.31) | data formatting | bytes 3981312 | tf_op jit(solution)/shard_map/cond/branch_1_fun/conv_general_dilated | solution.py:41
  329.5 2.5 slice_bitcast_fusion.1
  332.8 1.2 copy-done.3
  334.1 1.7 convert_reduce_fusion
  350.0 1.9 reshape.416
  352.1 7.1 %conditional.3 = (f32[64]{0:T(128)}, bf16[1,64,4096]{2,1,0:T(8,128)(2,1)}, f32[64,1728]{1,0:T(8,128)}, f32[64,1728]{1,0:T(8,128)}) conditional(s32[]{:T(128)} %bitcast.484, () %tuple.30, (bf16[2,64,20,20,20]{1,4,3,2,0:T(8,128)(2,1)}, bf16[64,1728]{1,0:T(8,128)(2,1)}, bf16[64,1728]{1,0:T(8,128)(2,1)}, f32[64]{0:T(128)S(1)}, ...), branch_computations={%region_5.6_spmd, %region_6.8_spmd} | conditional | flops 6641546240 | bytes 251059136 | solution.py:184
  354.2 0.9 stack.303.clone
  359.8 185.1 %psum.23 = f32[64]{0:T(128)S(1)} all-reduce(f32[64]{0:T(128)S(1)} %add.148), channel_id=1, replica_groups=mesh['groups'=2,'space'=16] {'space'}, use_global_device_ids=true, to_apply=%region_12.13 | all-reduce | flops 64 | bytes 512 | tf_op jit(solution)/shard_map/psum | solution.py:189
  545.5 2.0 add.146
  547.5 2.0 add.145
  549.5 2.3 pad_maximum_fusion.1
  551.8 87.1 %all-reduce.4.cloned.1.call-done = (f32[64,1728]{1,0:T(8,128)}, f32[64,1728]{1,0:T(8,128)}) async-done(((f32[64,1728]{1,0:T(8,128)}, f32[64,1728]{1,0:T(8,128)}), (f32[64,1728]{1,0:T(8,128)}, f32[64,1728]{1,0:T(8,128)})) %all-reduce.4.cloned.1.call-update) | async-done | bytes 884752 | tf_op jit(solution)/shard_map/psum | solution.py:189
  638.8 1.7 multiply_reduce_fusion
  640.6 1.7 multiply_reduce_fusion.1
  644.3 1.8 broadcast_multiply_fusion
  646.6 1.8 broadcast_multiply_fusion.1
  (148 shorter events, 50.0 us)
Async XLA Ops:
  7.2 2.2 copy-start.7
  7.2 631.7 %all-reduce.4.cloned.1.call-start = ((), (), s32[]{:S(2)}) async-start(), calls=%async_computation | async-start | bytes 1835008 | tf_op jit(solution)/shard_map/psum | solution.py:189
  11.1 6.7 %copy-start.26 = (s32[32,3]{0,1:T(4,128)S(1)}, s32[32,3]{0,1:T(4,128)}, u32[]{:S(2)}) copy-start(s32[32,3]{0,1:T(4,128)} %param.13) | copy-start | bytes 1156
  11.1 7.1 %copy-start.28 = (s32[27,3]{0,1:T(4,128)S(1)}, s32[27,3]{0,1:T(4,128)}, u32[]{:S(2)}) copy-start(s32[27,3]{0,1:T(4,128)} %constant.28.clone) | copy-start | bytes 976
  13.4 44.8 %collective-permute-start = (bf16[2,2,64,2,256]{2,4,3,1,0:T(8,128)(2,1)}, bf16[2,2,64,2,256]{2,4,3,1,0:T(8,128)(2,1)}, u32[]{:S(2)}, u32[]{:S(2)}) collective-permute-start(bf16[2,2,64,2,256]{2,4,3,1,0:T(8,128)(2,1)} %get-tuple-element.126), channel_id=1, source_target_pairs={{0,1},{1,2},{2,3},{3,4},{4,5},{5,6},{6,7},{7,8},{8,9},{9,10},{10,1... | collective-permute-start | bytes 786440 | tf_op jit(solution)/shard_map/ppermute | solution.py:24
  16.5 63.0 %collective-permute-start.1 = (bf16[2,2,64,2,256]{2,4,3,1,0:T(8,128)(2,1)}, bf16[2,2,64,2,256]{2,4,3,1,0:T(8,128)(2,1)}, u32[]{:S(2)}, u32[]{:S(2)}) collective-permute-start(bf16[2,2,64,2,256]{2,4,3,1,0:T(8,128)(2,1)} %get-tuple-element.127), channel_id=1, source_target_pairs={{1,0},{2,1},{3,2},{4,3},{5,4},{6,5},{7,6},{8,7},{9,8},{10,9},{11,1... | collective-permute-start | bytes 786440 | tf_op jit(solution)/shard_map/ppermute | solution.py:27
  19.0 3.7 copy-start.19
  28.1 2.1 copy-start.8
  32.1 4.5 copy-start.2
  149.1 43.3 %copy-start.21 = (bf16[64,1728]{1,0:T(8,128)(2,1)S(1)}, bf16[64,1728]{1,0:T(8,128)(2,1)}, u32[]{:S(2)}) copy-start(bf16[64,1728]{1,0:T(8,128)(2,1)} %param.16) | copy-start | bytes 663556
  149.1 43.3 %copy-start.23 = (bf16[64,1728]{1,0:T(8,128)(2,1)S(1)}, bf16[64,1728]{1,0:T(8,128)(2,1)}, u32[]{:S(2)}) copy-start(bf16[64,1728]{1,0:T(8,128)(2,1)} %param.14) | copy-start | bytes 663556
  149.1 43.3 %copy-start.27 = (f32[64]{0:T(128)S(1)}, f32[64]{0:T(128)}, u32[]{:S(2)}) copy-start(f32[64]{0:T(128)} %param.15) | copy-start | bytes 772
  192.4 159.6 %copy-start.20 = (pred[27,2]{0,1:T(4,128)(4,1)S(1)}, pred[27,2]{0,1:T(4,128)(4,1)}, u32[]{:S(2)}) copy-start(pred[27,2]{0,1:T(4,128)(4,1)} %copy-done.19) | copy-start | bytes 166
  193.2 57.0 %copy-start.13 = (f32[18,18,18]{2,1,0:T(8,128)}, f32[18,18,18]{2,1,0:T(8,128)S(1)}, u32[]{:S(2)}) copy-start(f32[18,18,18]{2,1,0:T(8,128)S(1)} %fusion.152) | copy-start | bytes 69988 | tf_op jit(solution)/shard_map/cond
  205.5 0.7 copy-start.31
  221.5 17.4 %copy-start.11 = (f32[18,18,8,3,64]{4,2,3,1,0:T(8,128)}, f32[18,18,8,3,64]{4,2,3,1,0:T(8,128)S(1)}, u32[]{:S(2)}) copy-start(f32[18,18,8,3,64]{4,2,3,1,0:T(8,128)S(1)} %broadcast_select_fusion) | copy-start | bytes 5971972 | tf_op jit(solution)/shard_map/cond
  260.5 0.7 copy-start.29
  268.0 1.7 copy-start.5
  278.0 7.4 %copy-start.14 = (f32[18,18,18]{2,1,0:T(8,128)S(1)}, f32[18,18,18]{2,1,0:T(8,128)}, u32[]{:S(2)}) copy-start(f32[18,18,18]{2,1,0:T(8,128)} %copy-done.13) | copy-start | bytes 69988 | tf_op jit(solution)/shard_map/cond
  312.9 5.3 copy-start.9
  322.2 9.9 %copy-start.24 = (f32[16,16,16]{2,1,0:T(8,128)S(1)}, f32[16,16,16]{2,1,0:T(8,128)}, u32[]{:S(2)}) copy-start(f32[16,16,16]{2,1,0:T(8,128)} %slice.1350) | copy-start | bytes 49156 | tf_op jit(solution)/shard_map/cond
  329.5 3.3 copy-start
  329.5 4.5 copy-start.3
  334.1 1.7 copy-start.17
Sparse Core Ops, SparseCore 0:
  549.6 89.1 all-reduce.3
where the time goes:
time: 668 us; the launch traced here: 656 us
  other arithmetic  195 us (29%)
  blocking collectives  185 us (28%)
  local copies, waits for them, and re-layouts  90.5 us (14%)
  waiting for transfers between devices  87.1 us (13%)
  matrix products  70.5 us (11%)
  between operations  17.8 us (3%)
    psum x1, blocking collectives, body(): lax.psum((grad_first, grad_second, grad_bias), 'space')  185 us
    psum x1, waiting for transfers between devices, body(): lax.psum((grad_first, grad_second, grad_bias), 'space')  87.1 us
    concatenate x2, other arithmetic, build_tile(): return jnp.concatenate(planes, axis=2)  86.5 us
    select_n x14, other arithmetic, build_tile(): jnp.where(matched[offset_index, 0], first_region, jnp.where(matched[offse...  71.5 us
    conv_general_dilated x3, matrix products, conv_valid(): lax.conv_general_dilated(inputs, kernel, (1, 1, 1), 'VALID', dimension_nu...  39 us
    conv_general_dilated x13, local copies, waits for them, and re-layouts, conv_valid(): lax.conv_general_dilated(inputs, kernel, (1, 1, 1), 'VALID', dimension_nu...  33.1 us
    dot_general x54, matrix products, filter_sums(): jnp.einsum('ou,iu->oi', flat_target, window, preferred_element_type=jnp.f...  31 us
  transfers between devices with their start and end apart: 3, of which 1 were waited for; matrix products, arithmetic and copies ran while one was open for 10% of the time, Pallas kernels for 0%

commit v1 on v0

v1 whole, which is shorter than its diff:
```python
import jax
import jax.numpy as jnp
import numpy as np
from jax import lax
from jax.experimental import pallas as pl
from jax.experimental.pallas import tpu as pltpu
from jax.sharding import PartitionSpec as P

CH = 64
BLOCK = 16
EDGE = 20
PLANE = 512
LANES = 384
SHIFTS = tuple(dy * EDGE + dz for dy in range(3) for dz in range(3))

neighbour_steps = (
    np.stack(np.meshgrid(np.arange(-1, 2), np.arange(-1, 2), np.arange(-1, 2), indexing="ij"), -1)
    .reshape(27, 3)
    .astype(np.int32)
)
clip_norm = 256.0


def plane_tables():
    lane = np.arange(LANES)
    y, z = lane // EDGE, lane % EDGE
    ry = (y >= 1).astype(int) + (y >= 17).astype(int)
    rz = (z >= 1).astype(int) + (z >= 17).astype(int)
    inside = (y < 18) & (z < 18)
    regions = ((ry * 3 + rz)[None, :] == np.arange(9)[:, None]) & inside[None, :]
    inner = (y >= 1) & (y <= 16) & (z >= 1) & (z <= 16)
    own = (y < 16) & (z < 16)
    compress = (y * 16 + z)[:, None] == np.arange(256)[None, :]
    compress = compress & own[:, None]
    return (
        regions.astype(np.float32),
        np.stack([inner, own]).astype(np.float32),
        compress.astype(np.float32),
    )


def shifted(plane, lanes):
    parts = []
    for s in SHIFTS:
        if plane.shape[1] > lanes:
            parts.append(plane[:, s : s + lanes])
        elif s == 0:
            parts.append(plane)
        else:
            parts.append(jnp.concatenate([plane[:, s:], plane[:, :s]], axis=1))
    return jnp.concatenate(parts, axis=0)


def block_kernel(
    active_ref,
    tile_ref,
    live_ref,
    masks_ref,
    compress_ref,
    w1_ref,
    w2t_ref,
    w1t_ref,
    bias_ref,
    grad_ref,
    first_ref,
    second_ref,
    gbias_ref,
    px,
    pre,
    back,
    gin,
    gown,
    spread,
):
    slot = pl.program_id(0)

    @pl.when(slot == 0)
    def _():
        first_ref[...] = jnp.zeros_like(first_ref)
        second_ref[...] = jnp.zeros_like(second_ref)
        gbias_ref[...] = jnp.zeros_like(gbias_ref)

    live = active_ref[slot] > 0

    @pl.when(jnp.logical_not(live))
    def _():
        grad_ref[...] = jnp.zeros_like(grad_ref)

    @pl.when(live)
    def _():
        own_mask = masks_ref[1:2, :] > 0
        inner_mask = masks_ref[0:1, :] > 0
        zero = jnp.zeros((CH, LANES), jnp.bfloat16)
        for k in (0, 1, 18, 19):
            gown[k] = zero
        for k in (0, 1, 2, 19, 20):
            gin[k] = zero

        def conv_step(p, carry):
            xp = shifted(tile_ref[0, p, 0:CH, :], LANES)
            px[p] = xp
            r1 = jnp.dot(w1_ref[...], xp, preferred_element_type=jnp.float32)
            pre[p + 2] = r1[0:CH]
            pre[p + 1] = pre[p + 1] + r1[CH : 2 * CH]
            pre[p] = pre[p] + r1[2 * CH :]
            gp = shifted(tile_ref[0, p, CH : 2 * CH, :], LANES)
            r2 = jnp.dot(w2t_ref[...], gp, preferred_element_type=jnp.float32)
            back[p + 2] = r2[0:CH]
            back[p + 1] = back[p + 1] + r2[CH : 2 * CH]
            back[p] = back[p] + r2[2 * CH :]
            return carry

        lax.fori_loop(0, EDGE, conv_step, 0)

        def own_step(x, carry):
            plane = tile_ref[0, x + 2, CH : 2 * CH, :]
            own = plane[:, 42 : 42 + LANES]
            gown[x + 2] = jnp.where(own_mask, own, jnp.zeros_like(own))
            return carry

        lax.fori_loop(0, 16, own_step, 0)

        def mid_step(x, carry):
            region = (x >= 1).astype(jnp.int32) + (x >= 17).astype(jnp.int32)
            on = live_ref[0, region] > 0
            value = pre[x + 2] + bias_ref[...]
            sig = 1.0 / (1.0 + jnp.exp(-value))
            hidden = jnp.where(on, value * sig, 0.0).astype(jnp.bfloat16)
            gpre = back[x + 2] * sig * (1.0 + value * (1.0 - sig))
            gpre = jnp.where(on, gpre, 0.0).astype(jnp.bfloat16)
            inner = jnp.where(inner_mask, gpre, jnp.zeros_like(gpre))

            @pl.when(jnp.logical_and(x >= 1, x <= 16))
            def _():
                gin[x + 2] = inner
                gbias_ref[...] += jnp.sum(inner.astype(jnp.float32), axis=1, keepdims=True)

            r3 = jnp.dot(w1t_ref[...], shifted(gpre, LANES), preferred_element_type=jnp.float32)
            spread[x + 2] = r3[0:CH]
            spread[x + 1] = spread[x + 1] + r3[CH : 2 * CH]
            spread[x] = spread[x] + r3[2 * CH :]
            left = jnp.concatenate([gown[x + 2], gown[x + 1], gown[x]], axis=0)
            second_ref[...] += lax.dot_general(
                left,
                shifted(hidden, LANES),
                (((1,), (1,)), ((), ())),
                preferred_element_type=jnp.float32,
            )
            return carry

        lax.fori_loop(0, 18, mid_step, 0)

        def first_step(t, carry):
            left = jnp.concatenate([gin[t + 2], gin[t + 1], gin[t]], axis=0)
            first_ref[...] += lax.dot_general(
                left, px[t], (((1,), (1,)), ((), ())), preferred_element_type=jnp.float32
            )
            return carry

        lax.fori_loop(1, 19, first_step, 0)

        for x in range(16):
            plane = tile_ref[0, x + 2, CH : 2 * CH, :]
            own = plane[:, 42 : 42 + LANES].astype(jnp.float32)
            total = (own + spread[x + 2]).astype(jnp.bfloat16)
            grad_ref[0, :, x * 256 : (x + 1) * 256] = jnp.dot(
                total, compress_ref[...], preferred_element_type=jnp.float32
            ).astype(jnp.bfloat16)


def block_grads(active, tiles, live, w1, w2t, w1t, bias):
    _, masks, compress = plane_tables()
    whole2 = lambda s, a: (0, 0)
    wide = pl.BlockSpec((3 * CH, 9 * CH), whole2)
    return pl.pallas_call(
        block_kernel,
        grid_spec=pltpu.PrefetchScalarGridSpec(
            num_scalar_prefetch=1,
            grid=(2,),
            in_specs=[
                pl.BlockSpec((1, EDGE, 2 * CH, PLANE), lambda s, a: (s, 0, 0, 0)),
                pl.BlockSpec((1, 3, 1, LANES), lambda s, a: (s, 0, 0, 0)),
                pl.BlockSpec((2, LANES), whole2),
                pl.BlockSpec((LANES, 256), whole2),
                wide,
                wide,
                wide,
                pl.BlockSpec((CH, 1), whole2),
            ],
            out_specs=[
                pl.BlockSpec((1, CH, BLOCK**3), lambda s, a: (s, 0, 0)),
                wide,
                wide,
                pl.BlockSpec((CH, 1), whole2),
            ],
            scratch_shapes=[
                pltpu.VMEM((EDGE, 9 * CH, LANES), jnp.bfloat16),
                pltpu.VMEM((22, CH, LANES), jnp.float32),
                pltpu.VMEM((22, CH, LANES), jnp.float32),
                pltpu.VMEM((21, CH, LANES), jnp.bfloat16),
                pltpu.VMEM((20, CH, LANES), jnp.bfloat16),
                pltpu.VMEM((20, CH, LANES), jnp.float32),
            ],
        ),
        out_shape=[
            jax.ShapeDtypeStruct((2, CH, BLOCK**3), jnp.bfloat16),
            jax.ShapeDtypeStruct((3 * CH, 9 * CH), jnp.float32),
            jax.ShapeDtypeStruct((3 * CH, 9 * CH), jnp.float32),
            jax.ShapeDtypeStruct((CH, 1), jnp.float32),
        ],
        compiler_params=pltpu.CompilerParams(vmem_limit_bytes=56 * 2**20),
    )(
        active,
        tiles,
        live,
        jnp.asarray(masks),
        jnp.asarray(compress, jnp.bfloat16),
        w1,
        w2t,
        w1t,
        bias,
    )


def slot_matches(nearby, slot_index):
    own_row = nearby[2 + slot_index]
    targets = own_row[None, :] + jnp.asarray(neighbour_steps)
    grouped = jnp.repeat(nearby.reshape(3, 2, 3), 9, axis=0)
    return jnp.all(grouped == targets[:, None, :], axis=2) & (grouped[:, :, 0] >= 0)


def placement(nearby):
    cell = jnp.arange(256)
    lane = jnp.arange(PLANE)
    rows = nearby.reshape(3, 2, 3)
    own = rows[1]
    dy = rows[:, None, :, 1] - own[None, :, None, 1]
    dz = rows[:, None, :, 2] - own[None, :, None, 2]
    good = (rows[:, None, :, 0] >= 0) & (jnp.abs(dy) <= 1) & (jnp.abs(dz) <= 1)
    ty = (cell // 16) + 16 * dy[..., None] + 2
    tz = (cell % 16) + 16 * dz[..., None] + 2
    fits = good[..., None] & (ty >= 0) & (ty < EDGE) & (tz >= 0) & (tz < EDGE)
    target = jnp.where(fits, ty * EDGE + tz, -1)
    return (target[..., None] == lane).astype(jnp.bfloat16)


def conv_matrix(weight, transposed):
    kernel = weight.reshape(CH, CH, 3, 9)
    if transposed:
        kernel = jnp.transpose(kernel[:, :, ::-1, ::-1], (2, 1, 3, 0))
    else:
        kernel = jnp.transpose(kernel, (2, 0, 3, 1))
    return kernel.reshape(3 * CH, 9 * CH)


def weight_layout(raw):
    return jnp.transpose(raw.reshape(3, CH, 9, CH), (1, 3, 0, 2)).reshape(CH, 27 * CH)


def place(planes, maps):
    return jnp.einsum(
        "kcxa,skat->sxct", planes, maps, preferred_element_type=jnp.float32
    ).astype(jnp.bfloat16)


def body(block_features, cotangent, coords, conv1_weight, conv1_bias, conv2_weight):
    slab_index = lax.axis_index("space")
    count = lax.axis_size("space")
    forward = [(i, i + 1) for i in range(count - 1)]
    backward = [(target, source) for source, target in forward]
    fields = jnp.concatenate([block_features, cotangent], axis=1)
    low = lax.ppermute(fields[:, :, 14 * 256 :], "space", forward)
    high = lax.ppermute(fields[:, :, : 2 * 256], "space", backward)
    padded_coords = jnp.pad(coords, ((2, 2), (0, 0)), constant_values=-1)
    nearby = lax.dynamic_slice_in_dim(padded_coords, slab_index * 2, 6, 0)
    active = (nearby[2:4, 0] >= 0).astype(jnp.int32)
    maps = placement(nearby)
    tiles = jnp.concatenate(
        [
            place(low.reshape(2, 2 * CH, 2, 256), maps[0]),
            place(fields.reshape(2, 2 * CH, 16, 256), maps[1]),
            place(high.reshape(2, 2 * CH, 2, 256), maps[2]),
        ],
        axis=1,
    )
    regions, _, _ = plane_tables()
    flags = jnp.stack(
        [jnp.any(slot_matches(nearby, s), axis=1).astype(jnp.float32) for s in range(2)]
    )
    live = jnp.sum(flags.reshape(2, 3, 9, 1) * regions[None, None], axis=2)
    grad_features, first, second, gbias = block_grads(
        active,
        tiles,
        live.reshape(2, 3, 1, LANES),
        conv_matrix(conv1_weight, False),
        conv_matrix(conv2_weight, True),
        conv_matrix(conv1_weight, True),
        conv1_bias.reshape(CH, 1),
    )
    raw_first, raw_second, raw_bias = lax.psum((first, second, gbias), "space")
    norm_total = jnp.sqrt(
        jnp.sum(raw_first * raw_first)
        + jnp.sum(raw_second * raw_second)
        + jnp.sum(raw_bias * raw_bias)
    )
    clip_scale = jnp.minimum(1.0, clip_norm / (norm_total + 1e-06))
    return (
        grad_features,
        weight_layout(clip_scale * raw_first),
        weight_layout(clip_scale * raw_second),
        (clip_scale * raw_bias).reshape(CH),
    )


def solution(mesh):
    placed = (
        P(("groups", "space"), None, None),
        P(("groups", "space"), None, None),
        P("groups", None),
        P(),
        P(),
        P(),
    )
    return jax.shard_map(
        body,
        mesh=mesh,
        in_specs=placed,
        out_specs=(
            P(("groups", "space"), None, None),
            P("groups", None),
            P("groups", None),
            P("groups"),
        ),
        check_vma=False,
    )
```

time: 668 us -> 234 us (0.35); the launches traced: 656 us -> 233 us
  other arithmetic: 195 us -> 17.2 us
  blocking collectives: 185 us -> 93 us
  local copies, waits for them, and re-layouts: 90.5 us -> 19 us
  matrix products: 70.5 us -> 9.48 us
  waiting for transfers between devices: 87.1 us -> 35.8 us
  Pallas kernels: 0 us -> 37.5 us
    psum x1, blocking collectives: 185 us -> 93 us  [body(): raw_first, raw_second, raw_bias = lax.psum((first, second, gbias), 'space')]
    concatenate x2 -> x3, other arithmetic: 86.5 us -> 9.08 us  [the longest x2 6.12 us: body(): fields = jnp.concatenate([block_features, cotangent], axis=1)]
    select_n x14 -> x2, other arithmetic: 71.5 us -> 0.11 us  [the longest x1 0.1 us: placement(): target = jnp.where(fits, ty * EDGE + tz, -1)]
    psum x1, waiting for transfers between devices: 87.1 us -> 35.8 us  [body(): raw_first, raw_second, raw_bias = lax.psum((first, second, gbias), 'space')]
    conv_general_dilated x3 -> x0, matrix products: 39 us -> none  [conv_valid(): lax.conv_general_dilated(inputs, kernel, (1, 1, 1), 'VALID', dimension_nu...]
    pallas_call x0 -> x1, Pallas kernels: none -> 37.5 us  [block_grads(): pl.pallas_call(block_kernel, grid_spec=pltpu.PrefetchScalarGridSpec(num_s...]
    conv_general_dilated x13 -> x0, local copies, waits for them, and re-layouts: 33.1 us -> none  [conv_valid(): lax.conv_general_dilated(inputs, kernel, (1, 1, 1), 'VALID', dimension_nu...]
    dot_general x57 -> x3, matrix products: 31.6 us -> 9.48 us  [place(): jnp.einsum('kcxa,skat->sxct', planes, maps, preferred_element_type=jnp.fl...]
  transfers between devices with their start and end apart: 3 -> 3, of which waited for: 1 -> 1; matrix products, arithmetic and copies ran while one was open for 10% -> 11% of each run, Pallas kernels for 0% -> 0%
where the time goes in v1:
time: 234 us; the launch traced here: 233 us
  blocking collectives  93 us (40%)
  Pallas kernels  37.5 us (16%)
  waiting for transfers between devices  35.8 us (15%)
  local copies, waits for them, and re-layouts  19 us (8%)
  other arithmetic  17.2 us (7%)
  between operations  16.4 us (7%)
  matrix products  9.48 us (4%)
  starting transfers between devices  5.07 us (2%)
    psum x1, blocking collectives, body(): raw_first, raw_second, raw_bias = lax.psum((first, second, gbias), 'space')  93 us
    pallas_call x1, Pallas kernels, block_grads(): pl.pallas_call(block_kernel, grid_spec=pltpu.PrefetchScalarGridSpec(num_s...  37.5 us
    psum x1, waiting for transfers between devices, body(): raw_first, raw_second, raw_bias = lax.psum((first, second, gbias), 'space')  35.8 us
    dot_general x3, matrix products, place(): jnp.einsum('kcxa,skat->sxct', planes, maps, preferred_element_type=jnp.fl...  9.48 us
    unnamed x28, local copies, waits for them, and re-layouts  6.62 us
    concatenate x2, other arithmetic, body(): fields = jnp.concatenate([block_features, cotangent], axis=1)  6.12 us
  transfers between devices with their start and end apart: 3, of which 1 were waited for; matrix products, arithmetic and copies ran while one was open for 11% of the time, Pallas kernels for 0%

profile of v1, /device:TPU:0, one launch (start us, length us, event | category | flops | bytes accessed | tf_op | source)
XLA Modules:
  0.0 233.4 jit_solution(12392389759518739798)
XLA Ops:
  7.2 2.1 copy.68
  9.3 1.8 copy.69
  11.2 2.0 fusion.9
  13.2 1.3 collective-permute-start.1
  14.5 3.8 %collective-permute-start = (bf16[2,128,512]{1,2,0:T(8,128)(2,1)S(1)}, bf16[2,128,512]{1,2,0:T(8,128)(2,1)}, u32[]{:S(2)}, u32[]{:S(2)}) collective-permute-start(bf16[2,128,512]{1,2,0:T(8,128)(2,1)S(1)} %get-tuple-element.28), channel_id=1, source_target_pairs={{0,1},{1,2},{2,3},{3,4},{4,5},{5,6},{6,7},{7,8},{8,9},{9,10},{10,1... | collective-permute-start | bytes 786440 | tf_op jit(solution)/shard_map/ppermute | solution.py:272
  18.3 0.1 copy.63
  18.4 0.1 compare_reduce_fusion.2
  18.7 4.1 %pad_maximum_fusion.1 = bf16[2,128,4096]{1,2,0:T(8,128)(2,1)} fusion(bf16[2,64,4096]{1,2,0:T(8,128)(2,1)} %copy.69, bf16[2,64,4096]{1,2,0:T(8,128)(2,1)S(1)} %copy.68), kind=kLoop, calls=%fused_computation.11 | loop fusion | flops 4194304 | bytes 4194304 | tf_op jit(solution)/shard_map/concatenate | solution.py:271
  22.8 0.2 slice_reduce_fusion.1
  23.0 0.1 copy.76
  23.1 0.1 copy.66
  23.2 0.1 copy.67
  23.3 0.1 copy.64
  23.4 0.1 copy.65
  23.6 0.1 compare_and_fusion
  23.7 0.1 and_select_fusion
  23.8 0.9 iota_compare_fusion
  24.8 0.1 eq.40
  24.9 0.1 eq.43
  25.0 0.1 compare_reduce_fusion.1
  25.1 0.1 reduce_and.23
  25.2 0.1 reshape.182
  25.3 0.1 reduce_and.25
  25.5 0.1 convert_element_type.57
  25.5 0.1 convert_element_type.56
  25.6 0.1 copy.78
  25.8 6.1 %fusion = bf16[2,16,128,512]{3,2,1,0:T(8,128)(2,1)} fusion(bf16[2,128,16,256,1]{1,3,2,0,4:T(8,128)(2,1)} %bitcast.120, pred[3,2,2,256,512]{3,4,2,1,0:T(32,128)(4,1)S(1)} %iota_compare_fusion), kind=kOutput, calls=%fused_computation.3 | convolution fusion | flops 2149580800 | bytes 6815744 | tf_op jit(solution)/shard_map/kcxa,skat->sxct/dot_general | solution.py:261
  31.8 0.6 fusion.13.active_ref
  32.4 0.1 multiply_reduce_fusion.2
  32.5 0.6 copy.84.live_ref
  33.1 0.3 copy.79
  33.4 0.2 reshape.184
  33.6 1.0 rev.7
  34.6 1.1 copy.115
  35.7 1.1 reshape.206.w1_ref
  36.8 0.3 copy.81
  37.0 0.2 reshape.186
  37.2 0.8 rev.6
  38.0 0.1 copy.116
  38.2 1.1 reshape.207.w2t_ref
  39.3 0.1 copy.117
  39.4 1.1 reshape.208.w1t_ref
  40.6 0.7 copy.88.bias_ref
  41.3 1.8 fusion.8
  43.1 1.6 fusion.7
  44.7 3.0 %pad_maximum_fusion.tile_ref = bf16[2,20,128,512]{3,2,1,0:T(8,128)(2,1)} fusion(bf16[2,2,128,512]{3,2,1,0:T(8,128)(2,1)S(1)} %fusion.8, bf16[2,16,128,512]{3,2,1,0:T(8,128)(2,1)S(1)} %copy-done, bf16[2,2,128,512]{3,2,1,0:T(8,128)(2,1)S(1)} %fusion.7), kind=kLoop, calls=%fused_computation.2 | loop fusion | flops 5242880 | bytes 10485760 | tf_op jit(solution)/shard_map/concatenate | solution.py:278
  47.7 37.5 %shard_map.129 = (bf16[2,64,4096]{2,1,0:T(8,128)(2,1)}, f32[192,576]{1,0:T(8,128)}, f32[192,576]{1,0:T(8,128)}, f32[64,1]{1,0:T(8,128)}) custom-call(s32[2]{0:T(128)} %fusion.13.active_ref, bf16[2,20,128,512]{3,2,1,0:T(8,128)(2,1)} %pad_maximum_fusion.tile_ref, f32[2,3,1,384]{3,2,1,0:T(1,128)} %copy.84.live_ref, f32[2,384]{1,0:T(2,128)} %constant.72.clone.masks_ref, ...), custom_call_target="tpu_custom_call" | custom-call | tf_op jit(solution)/shard_map/pallas_call | solution.py:175
  85.2 93.0 %psum.23 = f32[64,1]{1,0:T(8,128)S(1)} all-reduce(f32[64,1]{1,0:T(8,128)} %get-tuple-element.11), channel_id=1, replica_groups=mesh['groups'=2,'space'=16] {'space'}, use_global_device_ids=true, to_apply=%region_9.10 | all-reduce | flops 64 | bytes 512 | tf_op jit(solution)/shard_map/psum | solution.py:300
  178.2 0.6 multiply_reduce_fusion.4
  178.8 35.8 %all-reduce.4.cloned.1.call-done = (f32[192,576]{1,0:T(8,128)}, f32[192,576]{1,0:T(8,128)}) async-done(((f32[192,576]{1,0:T(8,128)}, f32[192,576]{1,0:T(8,128)}), (f32[192,576]{1,0:T(8,128)}, f32[192,576]{1,0:T(8,128)})) %all-reduce.4.cloned.1.call-update) | async-done | bytes 884752 | tf_op jit(solution)/shard_map/psum | solution.py:300
  214.6 1.8 multiply_reduce_fusion.1
  216.4 1.8 multiply_reduce_fusion
  220.2 1.1 broadcast_multiply_fusion.1
  221.3 0.6 multiply_reduce_fusion.3
  222.0 0.2 copy.89
  222.2 0.4 reshape.190
  222.6 0.6 copy.90
  223.1 0.1 reshape.191
  223.2 1.1 copy.93
  224.3 0.2 copy.91
  224.5 0.4 reshape.192
  224.9 0.6 copy.92
  225.4 0.1 reshape.193
  225.5 1.1 copy.94
  (37 shorter events, 0.6 us)
Async XLA Ops:
  7.2 2.2 copy-start.4
  7.2 207.4 %all-reduce.4.cloned.1.call-start = ((), (), s32[]{:S(2)}) async-start(), calls=%async_computation | async-start | bytes 1966080 | tf_op jit(solution)/shard_map/psum | solution.py:300
  11.2 7.1 %copy-start.9 = (s32[32,3]{0,1:T(4,128)S(1)}, s32[32,3]{0,1:T(4,128)}, u32[]{:S(2)}) copy-start(s32[32,3]{0,1:T(4,128)} %param.12) | copy-start | bytes 1156
  13.2 28.1 %collective-permute-start.1 = (bf16[2,128,512]{1,2,0:T(8,128)(2,1)}, bf16[2,128,512]{1,2,0:T(8,128)(2,1)}, u32[]{:S(2)}, u32[]{:S(2)}) collective-permute-start(bf16[2,128,512]{1,2,0:T(8,128)(2,1)} %get-tuple-element.29), channel_id=1, source_target_pairs={{1,0},{2,1},{3,2},{4,3},{5,4},{6,5},{7,6},{8,7},{9,8},{10,9},{11,1... | collective-permute-start | bytes 786440 | tf_op jit(solution)/shard_map/ppermute | solution.py:273
  14.5 28.6 %collective-permute-start = (bf16[2,128,512]{1,2,0:T(8,128)(2,1)S(1)}, bf16[2,128,512]{1,2,0:T(8,128)(2,1)}, u32[]{:S(2)}, u32[]{:S(2)}) collective-permute-start(bf16[2,128,512]{1,2,0:T(8,128)(2,1)S(1)} %get-tuple-element.28), channel_id=1, source_target_pairs={{0,1},{1,2},{2,3},{3,4},{4,5},{5,6},{6,7},{7,8},{8,9},{9,10},{10,1... | collective-permute-start | bytes 786440 | tf_op jit(solution)/shard_map/ppermute | solution.py:272
  18.7 6.0 %copy-start.8 = (s32[27,3]{0,1:T(4,128)S(1)}, s32[27,3]{0,1:T(4,128)}, u32[]{:S(2)}) copy-start(s32[27,3]{0,1:T(4,128)} %constant.70.clone) | copy-start | bytes 976
  24.7 7.1 %copy-start.2 = (pred[3,2,2,256,512]{3,4,2,1,0:T(32,128)(4,1)}, pred[3,2,2,256,512]{3,4,2,1,0:T(32,128)(4,1)S(1)}, u32[]{:S(2)}) copy-start(pred[3,2,2,256,512]{3,4,2,1,0:T(32,128)(4,1)S(1)} %iota_compare_fusion) | copy-start | bytes 4718596
  25.7 6.7 %copy-start.7 = (f32[9,384]{1,0:T(8,128)S(1)}, f32[9,384]{1,0:T(8,128)}, u32[]{:S(2)}) copy-start(f32[9,384]{1,0:T(8,128)} %constant.78) | copy-start | bytes 41476
  25.8 7.4 %copy-start.5 = (bf16[64,1728]{1,0:T(8,128)(2,1)S(1)}, bf16[64,1728]{1,0:T(8,128)(2,1)}, u32[]{:S(2)}) copy-start(bf16[64,1728]{1,0:T(8,128)(2,1)} %param.13) | copy-start | bytes 663556
  33.6 3.2 %copy-start.6 = (bf16[64,1728]{1,0:T(8,128)(2,1)S(1)}, bf16[64,1728]{1,0:T(8,128)(2,1)}, u32[]{:S(2)}) copy-start(bf16[64,1728]{1,0:T(8,128)(2,1)} %param.15) | copy-start | bytes 663556
  38.2 2.4 %copy-start.10 = (f32[64]{0:T(128)S(1)}, f32[64]{0:T(128)}, u32[]{:S(2)}) copy-start(f32[64]{0:T(128)} %param.14) | copy-start | bytes 772
  39.3 2.0 copy-start.3
  41.3 3.4 %copy-start = (bf16[2,16,128,512]{3,2,1,0:T(8,128)(2,1)S(1)}, bf16[2,16,128,512]{3,2,1,0:T(8,128)(2,1)}, u32[]{:S(2)}) copy-start(bf16[2,16,128,512]{3,2,1,0:T(8,128)(2,1)} %fusion) | copy-start | bytes 12582916
  214.6 6.7 %copy-start.1 = (f32[192,576]{1,0:T(8,128)S(1)}, f32[192,576]{1,0:T(8,128)}, u32[]{:S(2)}) copy-start(f32[192,576]{1,0:T(8,128)} %get-tuple-element.27) | copy-start | bytes 1327108
Sparse Core Ops, SparseCore 0:
  85.3 129.2 all-reduce.3

commit v2 on v1

--- a/solution.py
+++ b/solution.py
@@ -51,6 +51,12 @@
     return jnp.concatenate(parts, axis=0)
 
 
+def cell_sums(rows, columns):
+    return lax.dot_general(
+        rows, columns, (((1,), (1,)), ((), ())), preferred_element_type=jnp.float32
+    )
+
+
 def block_kernel(
     active_ref,
     tile_ref,
@@ -62,23 +68,24 @@
     w1t_ref,
     bias_ref,
     grad_ref,
-    first_ref,
-    second_ref,
-    gbias_ref,
+    sums_ref,
     px,
     pre,
     back,
     gin,
     gown,
     spread,
+    first,
+    second,
+    total_bias,
 ):
     slot = pl.program_id(0)
 
     @pl.when(slot == 0)
     def _():
-        first_ref[...] = jnp.zeros_like(first_ref)
-        second_ref[...] = jnp.zeros_like(second_ref)
-        gbias_ref[...] = jnp.zeros_like(gbias_ref)
+        first[...] = jnp.zeros_like(first)
+        second[...] = jnp.zeros_like(second)
+        total_bias[...] = jnp.zeros_like(total_bias)
 
     live = active_ref[slot] > 0
 
@@ -110,7 +117,7 @@
             back[p] = back[p] + r2[2 * CH :]
             return carry
 
-        lax.fori_loop(0, EDGE, conv_step, 0)
+        lax.fori_loop(0, EDGE, conv_step, 0, unroll=2)
 
         def own_step(x, carry):
             plane = tile_ref[0, x + 2, CH : 2 * CH, :]
@@ -118,7 +125,7 @@
             gown[x + 2] = jnp.where(own_mask, own, jnp.zeros_like(own))
             return carry
 
-        lax.fori_loop(0, 16, own_step, 0)
+        lax.fori_loop(0, 16, own_step, 0, unroll=4)
 
         def mid_step(x, carry):
             region = (x >= 1).astype(jnp.int32) + (x >= 17).astype(jnp.int32)
@@ -133,31 +140,26 @@
             @pl.when(jnp.logical_and(x >= 1, x <= 16))
             def _():
                 gin[x + 2] = inner
-                gbias_ref[...] += jnp.sum(inner.astype(jnp.float32), axis=1, keepdims=True)
 
             r3 = jnp.dot(w1t_ref[...], shifted(gpre, LANES), preferred_element_type=jnp.float32)
             spread[x + 2] = r3[0:CH]
             spread[x + 1] = spread[x + 1] + r3[CH : 2 * CH]
             spread[x] = spread[x] + r3[2 * CH :]
             left = jnp.concatenate([gown[x + 2], gown[x + 1], gown[x]], axis=0)
-            second_ref[...] += lax.dot_general(
-                left,
-                shifted(hidden, LANES),
-                (((1,), (1,)), ((), ())),
-                preferred_element_type=jnp.float32,
-            )
+            second[...] += cell_sums(shifted(hidden, LANES), left)
             return carry
 
-        lax.fori_loop(0, 18, mid_step, 0)
+        lax.fori_loop(0, 18, mid_step, 0, unroll=2)
+
+        ones = jnp.ones((16, LANES), jnp.bfloat16)
 
         def first_step(t, carry):
             left = jnp.concatenate([gin[t + 2], gin[t + 1], gin[t]], axis=0)
-            first_ref[...] += lax.dot_general(
-                left, px[t], (((1,), (1,)), ((), ())), preferred_element_type=jnp.float32
-            )
+            first[...] += cell_sums(px[t], left)
+            total_bias[...] += cell_sums(ones, left)
             return carry
 
-        lax.fori_loop(1, 19, first_step, 0)
+        lax.fori_loop(1, 19, first_step, 0, unroll=2)
 
         for x in range(16):
             plane = tile_ref[0, x + 2, CH : 2 * CH, :]
@@ -166,6 +168,12 @@
             grad_ref[0, :, x * 256 : (x + 1) * 256] = jnp.dot(
                 total, compress_ref[...], preferred_element_type=jnp.float32
             ).astype(jnp.bfloat16)
+
+    @pl.when(slot == 1)
+    def _():
+        sums_ref[0 : 9 * CH, :] = jnp.concatenate([first[...], second[...]], axis=1)
+        row = total_bias[0:8, :]
+        sums_ref[9 * CH :, :] = jnp.concatenate([row, row], axis=1)
 
 
 def block_grads(active, tiles, live, w1, w2t, w1t, bias):
@@ -189,9 +197,7 @@
             ],
             out_specs=[
                 pl.BlockSpec((1, CH, BLOCK**3), lambda s, a: (s, 0, 0)),
-                wide,
-                wide,
-                pl.BlockSpec((CH, 1), whole2),
+                pl.BlockSpec((9 * CH + 8, 6 * CH), whole2),
             ],
             scratch_shapes=[
                 pltpu.VMEM((EDGE, 9 * CH, LANES), jnp.bfloat16),
@@ -200,13 +206,14 @@
                 pltpu.VMEM((21, CH, LANES), jnp.bfloat16),
                 pltpu.VMEM((20, CH, LANES), jnp.bfloat16),
                 pltpu.VMEM((20, CH, LANES), jnp.float32),
+                pltpu.VMEM((9 * CH, 3 * CH), jnp.float32),
+                pltpu.VMEM((9 * CH, 3 * CH), jnp.float32),
+                pltpu.VMEM((16, 3 * CH), jnp.float32),
             ],
         ),
         out_shape=[
             jax.ShapeDtypeStruct((2, CH, BLOCK**3), jnp.bfloat16),
-            jax.ShapeDtypeStruct((3 * CH, 9 * CH), jnp.float32),
-            jax.ShapeDtypeStruct((3 * CH, 9 * CH), jnp.float32),
-            jax.ShapeDtypeStruct((CH, 1), jnp.float32),
+            jax.ShapeDtypeStruct((9 * CH + 8, 6 * CH), jnp.float32),
         ],
         compiler_params=pltpu.CompilerParams(vmem_limit_bytes=56 * 2**20),
     )(
@@ -254,7 +261,7 @@
 
 
 def weight_layout(raw):
-    return jnp.transpose(raw.reshape(3, CH, 9, CH), (1, 3, 0, 2)).reshape(CH, 27 * CH)
+    return jnp.transpose(raw.reshape(9, CH, 3, CH), (3, 1, 2, 0)).reshape(CH, 27 * CH)
 
 
 def place(planes, maps):
@@ -288,7 +295,7 @@
         [jnp.any(slot_matches(nearby, s), axis=1).astype(jnp.float32) for s in range(2)]
     )
     live = jnp.sum(flags.reshape(2, 3, 9, 1) * regions[None, None], axis=2)
-    grad_features, first, second, gbias = block_grads(
+    grad_features, sums = block_grads(
         active,
         tiles,
         live.reshape(2, 3, 1, LANES),
@@ -297,18 +304,17 @@
         conv_matrix(conv1_weight, True),
         conv1_bias.reshape(CH, 1),
     )
-    raw_first, raw_second, raw_bias = lax.psum((first, second, gbias), "space")
-    norm_total = jnp.sqrt(
-        jnp.sum(raw_first * raw_first)
-        + jnp.sum(raw_second * raw_second)
-        + jnp.sum(raw_bias * raw_bias)
-    )
+    sums = lax.psum(sums, "space")
+    raw = sums[: 9 * CH]
+    raw_bias = sums[9 * CH, :CH]
+    norm_total = jnp.sqrt(jnp.sum(raw * raw) + jnp.sum(raw_bias * raw_bias))
     clip_scale = jnp.minimum(1.0, clip_norm / (norm_total + 1e-06))
+    scaled = clip_scale * raw
     return (
         grad_features,
-        weight_layout(clip_scale * raw_first),
-        weight_layout(clip_scale * raw_second),
-        (clip_scale * raw_bias).reshape(CH),
+        weight_layout(scaled[:, : 3 * CH]),
+        weight_layout(scaled[:, 3 * CH :]),
+        clip_scale * raw_bias,
     )
 
 

time: 234 us -> 223 us (0.953)
  blocking collectives: 93 us -> 0 us
  waiting for transfers between devices: 35.8 us -> 123 us
  Pallas kernels: 37.5 us -> 33.4 us
    psum x1 -> x0, blocking collectives: 93 us -> none  [body(): raw_first, raw_second, raw_bias = lax.psum((first, second, gbias), 'space')]
    psum x1, waiting for transfers between devices: 35.8 us -> 123 us  [body(): sums = lax.psum(sums, 'space')]
    pallas_call x1, Pallas kernels: 37.5 us -> 33.4 us  [block_grads(): pl.pallas_call(block_kernel, grid_spec=pltpu.PrefetchScalarGridSpec(num_s...]
    unnamed x28 -> x26, local copies, waits for them, and re-layouts: 6.62 us -> 6.62 us
where the time goes in v2:
time: 223 us; the launch traced here: 222 us
  waiting for transfers between devices  123 us (55%)
  Pallas kernels  33.4 us (15%)
  local copies, waits for them, and re-layouts  18.8 us (8%)
  other arithmetic  17 us (8%)
  between operations  15.7 us (7%)
  matrix products  9.48 us (4%)
  starting transfers between devices  5.07 us (2%)
    psum x1, waiting for transfers between devices, body(): sums = lax.psum(sums, 'space')  123 us
    pallas_call x1, Pallas kernels, block_grads(): pl.pallas_call(block_kernel, grid_spec=pltpu.PrefetchScalarGridSpec(num_s...  33.4 us
    dot_general x3, matrix products, place(): jnp.einsum('kcxa,skat->sxct', planes, maps, preferred_element_type=jnp.fl...  9.48 us
    unnamed x26, local copies, waits for them, and re-layouts  6.62 us
    concatenate x2, other arithmetic, body(): fields = jnp.concatenate([block_features, cotangent], axis=1)  6.12 us
    reshape x6, local copies, waits for them, and re-layouts, conv_matrix(): return kernel.reshape(3 * CH, 9 * CH)  4.65 us
  transfers between devices with their start and end apart: 3, of which 1 were waited for; matrix products, arithmetic and copies ran while one was open for 11% of the time, Pallas kernels for 0%

profile of v2, /device:TPU:0, one launch (start us, length us, event | category | flops | bytes accessed | tf_op | source)
XLA Modules:
  0.0 222.4 jit_solution(10749106085275576886)
XLA Ops:
  7.2 2.1 copy.66
  9.3 1.8 copy.67
  11.2 2.0 fusion.9
  13.2 1.3 collective-permute-start.1
  14.5 3.8 %collective-permute-start = (bf16[2,128,512]{1,2,0:T(8,128)(2,1)S(1)}, bf16[2,128,512]{1,2,0:T(8,128)(2,1)}, u32[]{:S(2)}, u32[]{:S(2)}) collective-permute-start(bf16[2,128,512]{1,2,0:T(8,128)(2,1)S(1)} %get-tuple-element.22), channel_id=1, source_target_pairs={{0,1},{1,2},{2,3},{3,4},{4,5},{5,6},{6,7},{7,8},{8,9},{9,10},{10,1... | collective-permute-start | bytes 786440 | tf_op jit(solution)/shard_map/ppermute | solution.py:279
  18.2 0.1 pad_dynamic-slice_fusion
  18.3 0.1 copy.61
  18.4 0.1 compare_reduce_fusion.2
  18.6 0.1 fusion.15
  18.7 4.1 %pad_maximum_fusion.1 = bf16[2,128,4096]{1,2,0:T(8,128)(2,1)} fusion(bf16[2,64,4096]{1,2,0:T(8,128)(2,1)} %copy.67, bf16[2,64,4096]{1,2,0:T(8,128)(2,1)S(1)} %copy.66), kind=kLoop, calls=%fused_computation.11 | loop fusion | flops 4194304 | bytes 4194304 | tf_op jit(solution)/shard_map/concatenate | solution.py:278
  22.8 0.2 slice_reduce_fusion.1
  23.0 0.1 copy.74
  23.1 0.1 copy.64
  23.2 0.1 copy.65
  23.3 0.1 copy.62
  23.4 0.1 copy.63
  23.5 0.1 subtract_multiply_fusion
  23.6 0.1 compare_and_fusion
  23.7 0.1 and_select_fusion
  23.8 0.9 iota_compare_fusion
  24.8 0.1 eq.40
  24.9 0.1 eq.43
  25.0 0.1 compare_reduce_fusion.1
  25.1 0.1 reduce_and.23
  25.2 0.1 reshape.182
  25.3 0.1 reduce_and.25
  25.5 0.1 convert_element_type.57
  25.5 0.1 convert_element_type.56
  25.6 0.1 copy.76
  25.8 6.1 %fusion = bf16[2,16,128,512]{3,2,1,0:T(8,128)(2,1)} fusion(bf16[2,128,16,256,1]{1,3,2,0,4:T(8,128)(2,1)} %bitcast.118, pred[3,2,2,256,512]{3,4,2,1,0:T(32,128)(4,1)S(1)} %iota_compare_fusion), kind=kOutput, calls=%fused_computation.3 | convolution fusion | flops 2149580800 | bytes 6815744 | tf_op jit(solution)/shard_map/kcxa,skat->sxct/dot_general | solution.py:268
  31.8 0.6 fusion.13.active_ref
  32.4 0.1 multiply_reduce_fusion.1
  32.5 0.6 copy.82.live_ref
  33.1 0.3 copy.77
  33.4 0.2 reshape.184
  33.6 1.0 rev.7
  34.6 1.1 copy.111
  35.7 1.1 reshape.205.w1_ref
  36.8 0.3 copy.79
  37.0 0.2 reshape.186
  37.2 0.8 rev.6
  38.0 0.1 copy.112
  38.2 1.1 reshape.206.w2t_ref
  39.3 0.1 copy.113
  39.4 1.1 reshape.207.w1t_ref
  40.6 0.7 copy.86.bias_ref
  41.3 1.8 fusion.8
  43.1 1.6 fusion.7
  44.7 3.0 %pad_maximum_fusion.tile_ref = bf16[2,20,128,512]{3,2,1,0:T(8,128)(2,1)} fusion(bf16[2,2,128,512]{3,2,1,0:T(8,128)(2,1)S(1)} %fusion.8, bf16[2,16,128,512]{3,2,1,0:T(8,128)(2,1)S(1)} %copy-done, bf16[2,2,128,512]{3,2,1,0:T(8,128)(2,1)S(1)} %fusion.7), kind=kLoop, calls=%fused_computation.2 | loop fusion | flops 5242880 | bytes 10485760 | tf_op jit(solution)/shard_map/concatenate | solution.py:285
  47.7 33.4 %shard_map.129 = (bf16[2,64,4096]{2,1,0:T(8,128)(2,1)}, f32[584,384]{1,0:T(8,128)}) custom-call(s32[2]{0:T(128)} %fusion.13.active_ref, bf16[2,20,128,512]{3,2,1,0:T(8,128)(2,1)} %pad_maximum_fusion.tile_ref, f32[2,3,1,384]{3,2,1,0:T(1,128)} %copy.82.live_ref, f32[2,384]{1,0:T(2,128)} %constant.72.clone.masks_ref, ...), custom_call_target="tpu_custom_call" | custom-call | tf_op jit(solution)/shard_map/pallas_call | solution.py:183
  81.1 122.9 %all-reduce.3.cloned.1.call-done = f32[584,384]{1,0:T(8,128)} async-done(((f32[584,384]{1,0:T(8,128)}), f32[584,384]{1,0:T(8,128)}) %all-reduce.3.cloned.1.call-update) | async-done | bytes 897040 | tf_op jit(solution)/shard_map/psum | solution.py:307
  204.0 2.0 multiply_reduce_fusion
  206.0 1.3 multiply_reduce_fusion.2
  208.7 1.2 slice_multiply_fusion
  209.9 0.2 fusion.14
  210.1 0.4 reshape.190
  210.5 0.6 copy.87
  211.1 0.1 reshape.191
  211.2 1.1 copy.89
  212.2 0.4 reshape.192
  212.6 0.6 copy.88
  213.2 0.1 reshape.193
  213.3 1.1 copy.90
  214.3 1.2 multiply_bitcast_fusion
  (31 shorter events, 0.4 us)
Async XLA Ops:
  7.2 2.2 copy-start.3
  7.2 196.8 %all-reduce.3.cloned.1.call-start = ((), (), s32[]{:S(2)}) async-start(), calls=%async_computation | async-start | bytes 1794048 | tf_op jit(solution)/shard_map/psum | solution.py:307
  11.2 7.1 %copy-start.8 = (s32[32,3]{0,1:T(4,128)S(1)}, s32[32,3]{0,1:T(4,128)}, u32[]{:S(2)}) copy-start(s32[32,3]{0,1:T(4,128)} %param.12) | copy-start | bytes 1156
  13.2 28.1 %collective-permute-start.1 = (bf16[2,128,512]{1,2,0:T(8,128)(2,1)}, bf16[2,128,512]{1,2,0:T(8,128)(2,1)}, u32[]{:S(2)}, u32[]{:S(2)}) collective-permute-start(bf16[2,128,512]{1,2,0:T(8,128)(2,1)} %get-tuple-element.23), channel_id=1, source_target_pairs={{1,0},{2,1},{3,2},{4,3},{5,4},{6,5},{7,6},{8,7},{9,8},{10,9},{11,1... | collective-permute-start | bytes 786440 | tf_op jit(solution)/shard_map/ppermute | solution.py:280
  14.5 28.6 %collective-permute-start = (bf16[2,128,512]{1,2,0:T(8,128)(2,1)S(1)}, bf16[2,128,512]{1,2,0:T(8,128)(2,1)}, u32[]{:S(2)}, u32[]{:S(2)}) collective-permute-start(bf16[2,128,512]{1,2,0:T(8,128)(2,1)S(1)} %get-tuple-element.22), channel_id=1, source_target_pairs={{0,1},{1,2},{2,3},{3,4},{4,5},{5,6},{6,7},{7,8},{8,9},{9,10},{10,1... | collective-permute-start | bytes 786440 | tf_op jit(solution)/shard_map/ppermute | solution.py:279
  18.7 6.0 %copy-start.7 = (s32[27,3]{0,1:T(4,128)S(1)}, s32[27,3]{0,1:T(4,128)}, u32[]{:S(2)}) copy-start(s32[27,3]{0,1:T(4,128)} %constant.70.clone) | copy-start | bytes 976
  24.7 7.1 %copy-start.1 = (pred[3,2,2,256,512]{3,4,2,1,0:T(32,128)(4,1)}, pred[3,2,2,256,512]{3,4,2,1,0:T(32,128)(4,1)S(1)}, u32[]{:S(2)}) copy-start(pred[3,2,2,256,512]{3,4,2,1,0:T(32,128)(4,1)S(1)} %iota_compare_fusion) | copy-start | bytes 4718596
  25.7 6.7 %copy-start.6 = (f32[9,384]{1,0:T(8,128)S(1)}, f32[9,384]{1,0:T(8,128)}, u32[]{:S(2)}) copy-start(f32[9,384]{1,0:T(8,128)} %constant.78) | copy-start | bytes 41476
  25.8 7.4 %copy-start.4 = (bf16[64,1728]{1,0:T(8,128)(2,1)S(1)}, bf16[64,1728]{1,0:T(8,128)(2,1)}, u32[]{:S(2)}) copy-start(bf16[64,1728]{1,0:T(8,128)(2,1)} %param.13) | copy-start | bytes 663556
  33.6 3.2 %copy-start.5 = (bf16[64,1728]{1,0:T(8,128)(2,1)S(1)}, bf16[64,1728]{1,0:T(8,128)(2,1)}, u32[]{:S(2)}) copy-start(bf16[64,1728]{1,0:T(8,128)(2,1)} %param.15) | copy-start | bytes 663556
  38.2 2.4 %copy-start.9 = (f32[64]{0:T(128)S(1)}, f32[64]{0:T(128)}, u32[]{:S(2)}) copy-start(f32[64]{0:T(128)} %param.14) | copy-start | bytes 772
  39.3 2.0 copy-start.2
  41.3 3.4 %copy-start = (bf16[2,16,128,512]{3,2,1,0:T(8,128)(2,1)S(1)}, bf16[2,16,128,512]{3,2,1,0:T(8,128)(2,1)}, u32[]{:S(2)}) copy-start(bf16[2,16,128,512]{3,2,1,0:T(8,128)(2,1)} %fusion) | copy-start | bytes 12582916
Sparse Core Ops, SparseCore 0:
  81.2 122.7 all-reduce.2

commit v3 on v2

--- a/solution.py
+++ b/solution.py
@@ -270,6 +270,32 @@
     ).astype(jnp.bfloat16)
 
 
+def space_sum(values):
+    count = lax.axis_size("space")
+    if count & (count - 1):
+        return lax.psum(values, "space")
+    index = lax.axis_index("space")
+    steps = count.bit_length() - 1
+    rows = values.shape[0]
+    whole = -(-rows // (8 * count)) * 8 * count
+    held = jnp.pad(values, ((0, whole - rows), (0, 0)))
+    for step in range(steps):
+        pairs = [(i, i ^ (1 << step)) for i in range(count)]
+        upper = ((index >> step) & 1) == 1
+        half = held.shape[0] // 2
+        low, high = held[:half], held[half:]
+        sent = jnp.where(upper, low, high).astype(jnp.bfloat16)
+        got = lax.ppermute(sent, "space", pairs)
+        held = jnp.where(upper, high, low) + got.astype(jnp.float32)
+    held = held.astype(jnp.bfloat16)
+    for step in reversed(range(steps)):
+        pairs = [(i, i ^ (1 << step)) for i in range(count)]
+        upper = ((index >> step) & 1) == 1
+        got = lax.ppermute(held, "space", pairs)
+        held = jnp.concatenate([jnp.where(upper, got, held), jnp.where(upper, held, got)], axis=0)
+    return held[:rows].astype(jnp.float32)
+
+
 def body(block_features, cotangent, coords, conv1_weight, conv1_bias, conv2_weight):
     slab_index = lax.axis_index("space")
     count = lax.axis_size("space")
@@ -304,7 +330,7 @@
         conv_matrix(conv1_weight, True),
         conv1_bias.reshape(CH, 1),
     )
-    sums = lax.psum(sums, "space")
+    sums = space_sum(sums)
     raw = sums[: 9 * CH]
     raw_bias = sums[9 * CH, :CH]
     norm_total = jnp.sqrt(jnp.sum(raw * raw) + jnp.sum(raw_bias * raw_bias))

time: 223 us -> 148 us (0.66)
  waiting for transfers between devices: 123 us -> 22.7 us
  starting transfers between devices: 5.07 us -> 45.7 us
  between operations: 15.7 us -> 2.39 us
    psum x1 -> x0, waiting for transfers between devices: 123 us -> none  [body(): sums = lax.psum(sums, 'space')]
    ppermute x0 -> x8, starting transfers between devices: none -> 40.6 us  [the longest x4 36.1 us: space_sum(): got = lax.ppermute(sent, 'space', pairs)]
    ppermute x0 -> x8, waiting for transfers between devices: none -> 22.7 us  [the longest x4 11.5 us: space_sum(): got = lax.ppermute(sent, 'space', pairs)]
    unnamed x26 -> x28, local copies, waits for them, and re-layouts: 6.62 us -> 6.62 us
  transfers between devices with their start and end apart: 3 -> 10, of which waited for: 1 -> 8; matrix products, arithmetic and copies ran while one was open for 11% -> 17% of each run, Pallas kernels for 0% -> 0%
where the time goes in v3:
time: 148 us; the launch traced here: 147 us
  starting transfers between devices  45.7 us (31%)
  Pallas kernels  33.4 us (23%)
  waiting for transfers between devices  22.7 us (15%)
  local copies, waits for them, and re-layouts  18.8 us (13%)
  other arithmetic  15.1 us (10%)
  matrix products  9.49 us (6%)
  between operations  2.39 us (2%)
    ppermute x4, starting transfers between devices, space_sum(): got = lax.ppermute(sent, 'space', pairs)  36.1 us
    pallas_call x1, Pallas kernels, block_grads(): pl.pallas_call(block_kernel, grid_spec=pltpu.PrefetchScalarGridSpec(num_s...  33.4 us
    ppermute x4, waiting for transfers between devices, space_sum(): got = lax.ppermute(sent, 'space', pairs)  11.5 us
    ppermute x4, waiting for transfers between devices, space_sum(): got = lax.ppermute(held, 'space', pairs)  11.2 us
    dot_general x3, matrix products, place(): jnp.einsum('kcxa,skat->sxct', planes, maps, preferred_element_type=jnp.fl...  9.49 us
    unnamed x28, local copies, waits for them, and re-layouts  6.62 us
    concatenate x2, other arithmetic, body(): fields = jnp.concatenate([block_features, cotangent], axis=1)  6.12 us
    reshape x6, local copies, waits for them, and re-layouts, conv_matrix(): return kernel.reshape(3 * CH, 9 * CH)  4.63 us
  transfers between devices with their start and end apart: 10, of which 8 were waited for; matrix products, arithmetic and copies ran while one was open for 17% of the time, Pallas kernels for 0%

profile of v3, /device:TPU:0, one launch (start us, length us, event | category | flops | bytes accessed | tf_op | source)
XLA Modules:
  0.0 147.4 jit_solution(7680243978926881822)
XLA Ops:
  0.6 2.1 %copy.66 = bf16[2,64,4096]{1,2,0:T(8,128)(2,1)S(1)} copy(bf16[2,64,4096]{2,1,0:T(8,128)(2,1)} %param.10) | data formatting | bytes 2097152 | tf_op args[0]
  2.8 1.8 %copy.67 = bf16[2,64,4096]{1,2,0:T(8,128)(2,1)} copy(bf16[2,64,4096]{2,1,0:T(8,128)(2,1)S(1)} %copy-done.4) | data formatting | bytes 2097152 | tf_op args[1]
  4.6 2.0 %fusion.10 = (bf16[2,128,512]{1,2,0:T(8,128)(2,1)S(1)}, bf16[2,128,512]{1,2,0:T(8,128)(2,1)}) fusion(bf16[2,64,4096]{1,2,0:T(8,128)(2,1)S(1)} %copy.66, bf16[2,64,4096]{1,2,0:T(8,128)(2,1)} %copy.67), kind=kLoop, calls=%fused_computation.27 | loop fusion | flops 1048576 | bytes 2621440 | tf_op jit(solution)/shard_map/concatenate | solution.py:304
  6.6 1.3 collective-permute-start.1
  7.9 3.8 %collective-permute-start = (bf16[2,128,512]{1,2,0:T(8,128)(2,1)S(1)}, bf16[2,128,512]{1,2,0:T(8,128)(2,1)}, u32[]{:S(2)}, u32[]{:S(2)}) collective-permute-start(bf16[2,128,512]{1,2,0:T(8,128)(2,1)S(1)} %get-tuple-element.24), channel_id=1, source_target_pairs={{0,1},{1,2},{2,3},{3,4},{4,5},{5,6},{6,7},{7,8},{8,9},{9,10},{10,1... | collective-permute-start | bytes 786440 | tf_op jit(solution)/shard_map/ppermute | solution.py:305
  11.9 0.1 compare_reduce_fusion.2
  12.2 4.1 %pad_maximum_fusion.1 = bf16[2,128,4096]{1,2,0:T(8,128)(2,1)} fusion(bf16[2,64,4096]{1,2,0:T(8,128)(2,1)} %copy.67, bf16[2,64,4096]{1,2,0:T(8,128)(2,1)S(1)} %copy.66), kind=kLoop, calls=%fused_computation.11 | loop fusion | flops 4194304 | bytes 4194304 | tf_op jit(solution)/shard_map/concatenate | solution.py:304
  16.3 0.2 slice_reduce_fusion.1
  16.5 0.1 copy.74
  16.6 0.1 copy.64
  16.8 0.1 copy.62
  17.1 0.1 and_select_fusion
  17.3 0.9 iota_compare_fusion
  19.1 0.1 copy.76
  19.2 6.1 %fusion = bf16[2,16,128,512]{3,2,1,0:T(8,128)(2,1)} fusion(bf16[2,128,16,256,1]{1,3,2,0,4:T(8,128)(2,1)} %bitcast.118, pred[3,2,2,256,512]{3,4,2,1,0:T(32,128)(4,1)S(1)} %iota_compare_fusion), kind=kOutput, calls=%fused_computation.3 | convolution fusion | flops 2149580800 | bytes 6815744 | tf_op jit(solution)/shard_map/kcxa,skat->sxct/dot_general | solution.py:268
  25.3 0.6 fusion.14.active_ref
  25.9 0.1 multiply_reduce_fusion.1
  26.0 0.6 copy.82.live_ref
  26.6 0.3 copy.77
  26.9 0.2 reshape.184
  27.1 1.0 rev.7
  28.1 1.1 copy.111
  29.1 1.1 reshape.205.w1_ref
  30.2 0.3 copy.79
  30.5 0.2 reshape.186
  30.7 0.8 rev.6
  31.5 0.1 copy.112
  31.7 1.1 reshape.206.w2t_ref
  32.8 0.1 copy.113
  32.9 1.1 reshape.207.w1t_ref
  34.0 0.7 copy.86.bias_ref
  34.7 1.8 %fusion.8 = bf16[2,2,128,512]{3,2,1,0:T(8,128)(2,1)S(1)} fusion(bf16[2,128,2,256,1]{1,3,2,0,4:T(8,128)(2,1)} %bitcast.23, pred[3,2,2,256,512]{3,4,2,1,0:T(32,128)(4,1)S(1)} %copy-done.3), kind=kOutput, calls=%fused_computation.19 | convolution fusion | flops 268697600 | bytes 1310720 | tf_op jit(solution)/shard_map/kcxa,skat->sxct/dot_general | solution.py:268
  36.5 1.6 %fusion.7 = bf16[2,2,128,512]{3,2,1,0:T(8,128)(2,1)S(1)} fusion(bf16[2,128,2,256,1]{1,3,2,0,4:T(8,128)(2,1)} %bitcast.9, pred[3,2,2,256,512]{3,4,2,1,0:T(32,128)(4,1)S(1)} %copy-done.3), kind=kOutput, calls=%fused_computation.18 | convolution fusion | flops 268697600 | bytes 1310720 | tf_op jit(solution)/shard_map/kcxa,skat->sxct/dot_general | solution.py:268
  38.1 2.9 %pad_maximum_fusion.tile_ref = bf16[2,20,128,512]{3,2,1,0:T(8,128)(2,1)} fusion(bf16[2,2,128,512]{3,2,1,0:T(8,128)(2,1)S(1)} %fusion.8, bf16[2,16,128,512]{3,2,1,0:T(8,128)(2,1)S(1)} %copy-done.1, bf16[2,2,128,512]{3,2,1,0:T(8,128)(2,1)S(1)} %fusion.7), kind=kLoop, calls=%fused_computation.2 | loop fusion | flops 5242880 | bytes 10485760 | tf_op jit(solution)/shard_map/concatenate | solution.py:311
  41.1 33.4 %shard_map.129 = (bf16[2,64,4096]{2,1,0:T(8,128)(2,1)}, f32[584,384]{1,0:T(8,128)}) custom-call(s32[2]{0:T(128)} %fusion.14.active_ref, bf16[2,20,128,512]{3,2,1,0:T(8,128)(2,1)} %pad_maximum_fusion.tile_ref, f32[2,3,1,384]{3,2,1,0:T(1,128)} %copy.82.live_ref, f32[2,384]{1,0:T(2,128)} %constant.76.clone.masks_ref, ...), custom_call_target="tpu_custom_call" | custom-call | tf_op jit(solution)/shard_map/pallas_call | solution.py:183
  74.5 1.3 select_convert_fusion
  75.7 31.1 %collective-permute-start.2 = (bf16[320,384]{1,0:T(8,128)(2,1)S(1)}, bf16[320,384]{1,0:T(8,128)(2,1)S(1)}, u32[]{:S(2)}, u32[]{:S(2)}) collective-permute-start(bf16[320,384]{1,0:T(8,128)(2,1)S(1)} %select_convert_fusion), channel_id=1, source_target_pairs={{0,1},{1,0},{2,3},{3,2},{4,5},{5,4},{6,7},{7,6},{8,9},{9,8},{10,11... | collective-permute-start | bytes 737288 | tf_op jit(solution)/shard_map/ppermute | solution.py:288
  106.8 1.1 collective-permute-done.2
  108.1 2.4 %collective-permute-start.3 = (bf16[160,384]{1,0:T(8,128)(2,1)S(1)}, bf16[160,384]{1,0:T(8,128)(2,1)S(1)}, u32[]{:S(2)}, u32[]{:S(2)}) collective-permute-start(bf16[160,384]{1,0:T(8,128)(2,1)S(1)} %select_convert_fusion.1), channel_id=1, source_target_pairs={{0,2},{1,3},{2,0},{3,1},{4,6},{5,7},{6,4},{7,5},{8,10},{9,11},{10,... | collective-permute-start | bytes 368648 | tf_op jit(solution)/shard_map/ppermute | solution.py:288
  110.5 3.8 %collective-permute-done.3 = bf16[160,384]{1,0:T(8,128)(2,1)S(1)} collective-permute-done((bf16[160,384]{1,0:T(8,128)(2,1)S(1)}, bf16[160,384]{1,0:T(8,128)(2,1)S(1)}, u32[]{:S(2)}, u32[]{:S(2)}) %collective-permute-start.3) | collective-permute-done | bytes 122912 | tf_op jit(solution)/shard_map/ppermute | solution.py:288
  114.4 1.6 %collective-permute-start.4 = (bf16[80,384]{1,0:T(8,128)(2,1)S(1)}, bf16[80,384]{1,0:T(8,128)(2,1)S(1)}, u32[]{:S(2)}, u32[]{:S(2)}) collective-permute-start(bf16[80,384]{1,0:T(8,128)(2,1)S(1)} %select_convert_fusion.2), channel_id=1, source_target_pairs={{0,4},{1,5},{2,6},{3,7},{4,0},{5,1},{6,2},{7,3},{8,12},{9,13},{10,... | collective-permute-start | bytes 184328 | tf_op jit(solution)/shard_map/ppermute | solution.py:288
  116.0 2.6 %collective-permute-done.4 = bf16[80,384]{1,0:T(8,128)(2,1)S(1)} collective-permute-done((bf16[80,384]{1,0:T(8,128)(2,1)S(1)}, bf16[80,384]{1,0:T(8,128)(2,1)S(1)}, u32[]{:S(2)}, u32[]{:S(2)}) %collective-permute-start.4) | collective-permute-done | bytes 61472 | tf_op jit(solution)/shard_map/ppermute | solution.py:288
  118.7 0.9 collective-permute-start.5
  119.7 3.9 %collective-permute-done.5 = bf16[40,384]{1,0:T(8,128)(2,1)S(1)} collective-permute-done((bf16[40,384]{1,0:T(8,128)(2,1)S(1)}, bf16[40,384]{1,0:T(8,128)(2,1)S(1)}, u32[]{:S(2)}, u32[]{:S(2)}) %collective-permute-start.5) | collective-permute-done | bytes 30752 | tf_op jit(solution)/shard_map/ppermute | solution.py:288
  123.6 0.9 collective-permute-start.6
  124.5 3.9 %collective-permute-done.6 = bf16[40,384]{1,0:T(8,128)(2,1)S(1)} collective-permute-done((bf16[40,384]{1,0:T(8,128)(2,1)S(1)}, bf16[40,384]{1,0:T(8,128)(2,1)S(1)}, u32[]{:S(2)}, u32[]{:S(2)}) %collective-permute-start.6) | collective-permute-done | bytes 30752 | tf_op jit(solution)/shard_map/ppermute | solution.py:294
  128.5 1.6 %collective-permute-start.7 = (bf16[80,384]{1,0:T(8,128)(2,1)S(1)}, bf16[80,384]{1,0:T(8,128)(2,1)S(1)}, u32[]{:S(2)}, u32[]{:S(2)}) collective-permute-start(bf16[80,384]{1,0:T(8,128)(2,1)S(1)} %pad_maximum_fusion.5), channel_id=1, source_target_pairs={{0,4},{1,5},{2,6},{3,7},{4,0},{5,1},{6,2},{7,3},{8,12},{9,13},{10,... | collective-permute-start | bytes 184328 | tf_op jit(solution)/shard_map/ppermute | solution.py:294
  130.1 2.7 %collective-permute-done.7 = bf16[80,384]{1,0:T(8,128)(2,1)S(1)} collective-permute-done((bf16[80,384]{1,0:T(8,128)(2,1)S(1)}, bf16[80,384]{1,0:T(8,128)(2,1)S(1)}, u32[]{:S(2)}, u32[]{:S(2)}) %collective-permute-start.7) | collective-permute-done | bytes 61472 | tf_op jit(solution)/shard_map/ppermute | solution.py:294
  132.8 1.9 %collective-permute-start.8 = (bf16[160,384]{1,0:T(8,128)(2,1)S(1)}, bf16[160,384]{1,0:T(8,128)(2,1)S(1)}, u32[]{:S(2)}, u32[]{:S(2)}) collective-permute-start(bf16[160,384]{1,0:T(8,128)(2,1)S(1)} %pad_maximum_fusion.4), channel_id=1, source_target_pairs={{0,2},{1,3},{2,0},{3,1},{4,6},{5,7},{6,4},{7,5},{8,10},{9,11},{10,... | collective-permute-start | bytes 368648 | tf_op jit(solution)/shard_map/ppermute | solution.py:294
  134.7 3.1 %collective-permute-done.8 = bf16[160,384]{1,0:T(8,128)(2,1)S(1)} collective-permute-done((bf16[160,384]{1,0:T(8,128)(2,1)S(1)}, bf16[160,384]{1,0:T(8,128)(2,1)S(1)}, u32[]{:S(2)}, u32[]{:S(2)}) %collective-permute-start.8) | collective-permute-done | bytes 122912 | tf_op jit(solution)/shard_map/ppermute | solution.py:294
  138.0 1.5 %collective-permute-done.9 = bf16[320,384]{1,0:T(8,128)(2,1)S(1)} collective-permute-done((bf16[320,384]{1,0:T(8,128)(2,1)S(1)}, bf16[320,384]{1,0:T(8,128)(2,1)S(1)}, u32[]{:S(2)}, u32[]{:S(2)}) %collective-permute-start.9) | collective-permute-done | bytes 245792 | tf_op jit(solution)/shard_map/ppermute | solution.py:294
  139.5 0.1 broadcast_select_fusion.1
  139.6 0.6 fusion.15
  140.2 0.8 multiply_reduce_fusion
  142.5 0.2 fusion.17
  142.7 0.4 reshape.190
  143.1 0.6 copy.87
  143.7 0.1 reshape.191
  143.8 1.1 copy.89
  144.8 0.4 reshape.192
  145.2 0.6 copy.88
  145.8 0.1 reshape.193
  145.9 1.1 copy.90
  146.9 0.5 fusion.16
  (62 shorter events, 2.1 us)
Async XLA Ops:
  0.6 2.1 %copy-start.4 = (bf16[2,64,4096]{2,1,0:T(8,128)(2,1)S(1)}, bf16[2,64,4096]{2,1,0:T(8,128)(2,1)}, u32[]{:S(2)}) copy-start(bf16[2,64,4096]{2,1,0:T(8,128)(2,1)} %param.11) | copy-start | bytes 3145732
  4.6 7.1 %copy-start.9 = (s32[32,3]{0,1:T(4,128)S(1)}, s32[32,3]{0,1:T(4,128)}, u32[]{:S(2)}) copy-start(s32[32,3]{0,1:T(4,128)} %param.12) | copy-start | bytes 1156
  6.6 28.1 %collective-permute-start.1 = (bf16[2,128,512]{1,2,0:T(8,128)(2,1)}, bf16[2,128,512]{1,2,0:T(8,128)(2,1)}, u32[]{:S(2)}, u32[]{:S(2)}) collective-permute-start(bf16[2,128,512]{1,2,0:T(8,128)(2,1)} %get-tuple-element.25), channel_id=1, source_target_pairs={{1,0},{2,1},{3,2},{4,3},{5,4},{6,5},{7,6},{8,7},{9,8},{10,9},{11,1... | collective-permute-start | bytes 786440 | tf_op jit(solution)/shard_map/ppermute | solution.py:306
  7.9 28.6 %collective-permute-start = (bf16[2,128,512]{1,2,0:T(8,128)(2,1)S(1)}, bf16[2,128,512]{1,2,0:T(8,128)(2,1)}, u32[]{:S(2)}, u32[]{:S(2)}) collective-permute-start(bf16[2,128,512]{1,2,0:T(8,128)(2,1)S(1)} %get-tuple-element.24), channel_id=1, source_target_pairs={{0,1},{1,2},{2,3},{3,4},{4,5},{5,6},{6,7},{7,8},{8,9},{9,10},{10,1... | collective-permute-start | bytes 786440 | tf_op jit(solution)/shard_map/ppermute | solution.py:305
  12.2 6.0 %copy-start.8 = (s32[27,3]{0,1:T(4,128)S(1)}, s32[27,3]{0,1:T(4,128)}, u32[]{:S(2)}) copy-start(s32[27,3]{0,1:T(4,128)} %constant.74.clone) | copy-start | bytes 976
  18.2 7.1 %copy-start.2 = (pred[3,2,2,256,512]{3,4,2,1,0:T(32,128)(4,1)}, pred[3,2,2,256,512]{3,4,2,1,0:T(32,128)(4,1)S(1)}, u32[]{:S(2)}) copy-start(pred[3,2,2,256,512]{3,4,2,1,0:T(32,128)(4,1)S(1)} %iota_compare_fusion) | copy-start | bytes 4718596
  19.2 6.7 %copy-start.7 = (f32[9,384]{1,0:T(8,128)S(1)}, f32[9,384]{1,0:T(8,128)}, u32[]{:S(2)}) copy-start(f32[9,384]{1,0:T(8,128)} %constant.84) | copy-start | bytes 41476
  19.2 7.4 %copy-start.5 = (bf16[64,1728]{1,0:T(8,128)(2,1)S(1)}, bf16[64,1728]{1,0:T(8,128)(2,1)}, u32[]{:S(2)}) copy-start(bf16[64,1728]{1,0:T(8,128)(2,1)} %param.13) | copy-start | bytes 663556
  27.1 3.2 %copy-start.6 = (bf16[64,1728]{1,0:T(8,128)(2,1)S(1)}, bf16[64,1728]{1,0:T(8,128)(2,1)}, u32[]{:S(2)}) copy-start(bf16[64,1728]{1,0:T(8,128)(2,1)} %param.15) | copy-start | bytes 663556
  31.6 2.4 %copy-start.10 = (f32[64]{0:T(128)S(1)}, f32[64]{0:T(128)}, u32[]{:S(2)}) copy-start(f32[64]{0:T(128)} %param.14) | copy-start | bytes 772
  32.8 1.9 %copy-start.3 = (pred[3,2,2,256,512]{3,4,2,1,0:T(32,128)(4,1)S(1)}, pred[3,2,2,256,512]{3,4,2,1,0:T(32,128)(4,1)}, u32[]{:S(2)}) copy-start(pred[3,2,2,256,512]{3,4,2,1,0:T(32,128)(4,1)} %copy-done.2) | copy-start | bytes 4718596
  34.7 3.4 %copy-start.1 = (bf16[2,16,128,512]{3,2,1,0:T(8,128)(2,1)S(1)}, bf16[2,16,128,512]{3,2,1,0:T(8,128)(2,1)}, u32[]{:S(2)}) copy-start(bf16[2,16,128,512]{3,2,1,0:T(8,128)(2,1)} %fusion) | copy-start | bytes 12582916
  74.5 33.5 %copy-start = (f32[584,384]{1,0:T(8,128)S(1)}, f32[584,384]{1,0:T(8,128)}, u32[]{:S(2)}) copy-start(f32[584,384]{1,0:T(8,128)} %get-tuple-element.7) | copy-start | bytes 2691076
  75.7 32.2 %collective-permute-start.2 = (bf16[320,384]{1,0:T(8,128)(2,1)S(1)}, bf16[320,384]{1,0:T(8,128)(2,1)S(1)}, u32[]{:S(2)}, u32[]{:S(2)}) collective-permute-start(bf16[320,384]{1,0:T(8,128)(2,1)S(1)} %select_convert_fusion), channel_id=1, source_target_pairs={{0,1},{1,0},{2,3},{3,2},{4,5},{5,4},{6,7},{7,6},{8,9},{9,8},{10,11... | collective-permute-start | bytes 737288 | tf_op jit(solution)/shard_map/ppermute | solution.py:288
  108.1 6.3 %collective-permute-start.3 = (bf16[160,384]{1,0:T(8,128)(2,1)S(1)}, bf16[160,384]{1,0:T(8,128)(2,1)S(1)}, u32[]{:S(2)}, u32[]{:S(2)}) collective-permute-start(bf16[160,384]{1,0:T(8,128)(2,1)S(1)} %select_convert_fusion.1), channel_id=1, source_target_pairs={{0,2},{1,3},{2,0},{3,1},{4,6},{5,7},{6,4},{7,5},{8,10},{9,11},{10,... | collective-permute-start | bytes 368648 | tf_op jit(solution)/shard_map/ppermute | solution.py:288
  114.4 4.3 %collective-permute-start.4 = (bf16[80,384]{1,0:T(8,128)(2,1)S(1)}, bf16[80,384]{1,0:T(8,128)(2,1)S(1)}, u32[]{:S(2)}, u32[]{:S(2)}) collective-permute-start(bf16[80,384]{1,0:T(8,128)(2,1)S(1)} %select_convert_fusion.2), channel_id=1, source_target_pairs={{0,4},{1,5},{2,6},{3,7},{4,0},{5,1},{6,2},{7,3},{8,12},{9,13},{10,... | collective-permute-start | bytes 184328 | tf_op jit(solution)/shard_map/ppermute | solution.py:288
  118.7 4.9 %collective-permute-start.5 = (bf16[40,384]{1,0:T(8,128)(2,1)S(1)}, bf16[40,384]{1,0:T(8,128)(2,1)S(1)}, u32[]{:S(2)}, u32[]{:S(2)}) collective-permute-start(bf16[40,384]{1,0:T(8,128)(2,1)S(1)} %select_convert_fusion.3), channel_id=1, source_target_pairs={{0,8},{1,9},{2,10},{3,11},{4,12},{5,13},{6,14},{7,15},{8,0},{9,1},... | collective-permute-start | bytes 92168 | tf_op jit(solution)/shard_map/ppermute | solution.py:288
  123.6 4.9 %collective-permute-start.6 = (bf16[40,384]{1,0:T(8,128)(2,1)S(1)}, bf16[40,384]{1,0:T(8,128)(2,1)S(1)}, u32[]{:S(2)}, u32[]{:S(2)}) collective-permute-start(bf16[40,384]{1,0:T(8,128)(2,1)S(1)} %add_convert_fusion), channel_id=1, source_target_pairs={{0,8},{1,9},{2,10},{3,11},{4,12},{5,13},{6,14},{7,15},{8,0},{9,1},... | collective-permute-start | bytes 92168 | tf_op jit(solution)/shard_map/ppermute | solution.py:294
  128.5 4.3 %collective-permute-start.7 = (bf16[80,384]{1,0:T(8,128)(2,1)S(1)}, bf16[80,384]{1,0:T(8,128)(2,1)S(1)}, u32[]{:S(2)}, u32[]{:S(2)}) collective-permute-start(bf16[80,384]{1,0:T(8,128)(2,1)S(1)} %pad_maximum_fusion.5), channel_id=1, source_target_pairs={{0,4},{1,5},{2,6},{3,7},{4,0},{5,1},{6,2},{7,3},{8,12},{9,13},{10,... | collective-permute-start | bytes 184328 | tf_op jit(solution)/shard_map/ppermute | solution.py:294
  132.8 4.9 %collective-permute-start.8 = (bf16[160,384]{1,0:T(8,128)(2,1)S(1)}, bf16[160,384]{1,0:T(8,128)(2,1)S(1)}, u32[]{:S(2)}, u32[]{:S(2)}) collective-permute-start(bf16[160,384]{1,0:T(8,128)(2,1)S(1)} %pad_maximum_fusion.4), channel_id=1, source_target_pairs={{0,2},{1,3},{2,0},{3,1},{4,6},{5,7},{6,4},{7,5},{8,10},{9,11},{10,... | collective-permute-start | bytes 368648 | tf_op jit(solution)/shard_map/ppermute | solution.py:294
  137.9 1.6 %collective-permute-start.9 = (bf16[320,384]{1,0:T(8,128)(2,1)S(1)}, bf16[320,384]{1,0:T(8,128)(2,1)S(1)}, u32[]{:S(2)}, u32[]{:S(2)}) collective-permute-start(bf16[320,384]{1,0:T(8,128)(2,1)S(1)} %pad_maximum_fusion.3), channel_id=1, source_target_pairs={{0,1},{1,0},{2,3},{3,2},{4,5},{5,4},{6,7},{7,6},{8,9},{9,8},{10,11... | collective-permute-start | bytes 737288 | tf_op jit(solution)/shard_map/ppermute | solution.py:294

commit v4 on v3

--- a/solution.py
+++ b/solution.py
@@ -117,7 +117,7 @@
             back[p] = back[p] + r2[2 * CH :]
             return carry
 
-        lax.fori_loop(0, EDGE, conv_step, 0, unroll=2)
+        lax.fori_loop(0, EDGE, conv_step, 0, unroll=4)
 
         def own_step(x, carry):
             plane = tile_ref[0, x + 2, CH : 2 * CH, :]
@@ -149,7 +149,7 @@
             second[...] += cell_sums(shifted(hidden, LANES), left)
             return carry
 
-        lax.fori_loop(0, 18, mid_step, 0, unroll=2)
+        lax.fori_loop(0, 18, mid_step, 0, unroll=3)
 
         ones = jnp.ones((16, LANES), jnp.bfloat16)
 
@@ -159,7 +159,7 @@
             total_bias[...] += cell_sums(ones, left)
             return carry
 
-        lax.fori_loop(1, 19, first_step, 0, unroll=2)
+        lax.fori_loop(1, 19, first_step, 0, unroll=3)
 
         for x in range(16):
             plane = tile_ref[0, x + 2, CH : 2 * CH, :]

time: 148 us -> 144 us (0.973)
  waiting for transfers between devices: 22.7 us -> 19.7 us
  Pallas kernels: 33.4 us -> 31.4 us
    ppermute x4, starting transfers between devices: 4.52 us -> 6.82 us  [space_sum(): got = lax.ppermute(held, 'space', pairs)]
    ppermute x4, waiting for transfers between devices: 11.2 us -> 8.95 us  [space_sum(): got = lax.ppermute(held, 'space', pairs)]
    pallas_call x1, Pallas kernels: 33.4 us -> 31.4 us  [block_grads(): pl.pallas_call(block_kernel, grid_spec=pltpu.PrefetchScalarGridSpec(num_s...]
    ppermute x4, starting transfers between devices: 36.1 us -> 34.5 us  [space_sum(): got = lax.ppermute(sent, 'space', pairs)]
where the time goes in v4:
time: 144 us; the launch traced here: 143 us
  starting transfers between devices  46.3 us (32%)
  Pallas kernels  31.4 us (22%)
  waiting for transfers between devices  19.7 us (14%)
  local copies, waits for them, and re-layouts  18.8 us (13%)
  other arithmetic  15.1 us (10%)
  matrix products  9.49 us (7%)
  between operations  2.4 us (2%)
    ppermute x4, starting transfers between devices, space_sum(): got = lax.ppermute(sent, 'space', pairs)  34.5 us
    pallas_call x1, Pallas kernels, block_grads(): pl.pallas_call(block_kernel, grid_spec=pltpu.PrefetchScalarGridSpec(num_s...  31.4 us
    ppermute x4, waiting for transfers between devices, space_sum(): got = lax.ppermute(sent, 'space', pairs)  10.8 us
    dot_general x3, matrix products, place(): jnp.einsum('kcxa,skat->sxct', planes, maps, preferred_element_type=jnp.fl...  9.49 us
    ppermute x4, waiting for transfers between devices, space_sum(): got = lax.ppermute(held, 'space', pairs)  8.95 us
    ppermute x4, starting transfers between devices, space_sum(): got = lax.ppermute(held, 'space', pairs)  6.82 us
    unnamed x28, local copies, waits for them, and re-layouts  6.62 us
    concatenate x2, other arithmetic, body(): fields = jnp.concatenate([block_features, cotangent], axis=1)  6.12 us
  transfers between devices with their start and end apart: 10, of which 8 were waited for; matrix products, arithmetic and copies ran while one was open for 17% of the time, Pallas kernels for 0%

profile of v4, /device:TPU:0, one launch (start us, length us, event | category | flops | bytes accessed | tf_op | source)
XLA Modules:
  0.0 143.2 jit_solution(5872210313191791508)
XLA Ops:
  0.6 2.1 %copy.66 = bf16[2,64,4096]{1,2,0:T(8,128)(2,1)S(1)} copy(bf16[2,64,4096]{2,1,0:T(8,128)(2,1)} %param.10) | data formatting | bytes 2097152 | tf_op args[0]
  2.8 1.8 %copy.67 = bf16[2,64,4096]{1,2,0:T(8,128)(2,1)} copy(bf16[2,64,4096]{2,1,0:T(8,128)(2,1)S(1)} %copy-done.4) | data formatting | bytes 2097152 | tf_op args[1]
  4.6 2.0 %fusion.10 = (bf16[2,128,512]{1,2,0:T(8,128)(2,1)S(1)}, bf16[2,128,512]{1,2,0:T(8,128)(2,1)}) fusion(bf16[2,64,4096]{1,2,0:T(8,128)(2,1)S(1)} %copy.66, bf16[2,64,4096]{1,2,0:T(8,128)(2,1)} %copy.67), kind=kLoop, calls=%fused_computation.27 | loop fusion | flops 1048576 | bytes 2621440 | tf_op jit(solution)/shard_map/concatenate | solution.py:304
  6.6 1.3 collective-permute-start.1
  7.9 3.8 %collective-permute-start = (bf16[2,128,512]{1,2,0:T(8,128)(2,1)S(1)}, bf16[2,128,512]{1,2,0:T(8,128)(2,1)}, u32[]{:S(2)}, u32[]{:S(2)}) collective-permute-start(bf16[2,128,512]{1,2,0:T(8,128)(2,1)S(1)} %get-tuple-element.24), channel_id=1, source_target_pairs={{0,1},{1,2},{2,3},{3,4},{4,5},{5,6},{6,7},{7,8},{8,9},{9,10},{10,1... | collective-permute-start | bytes 786440 | tf_op jit(solution)/shard_map/ppermute | solution.py:305
  11.9 0.1 compare_reduce_fusion.2
  12.2 4.1 %pad_maximum_fusion.1 = bf16[2,128,4096]{1,2,0:T(8,128)(2,1)} fusion(bf16[2,64,4096]{1,2,0:T(8,128)(2,1)} %copy.67, bf16[2,64,4096]{1,2,0:T(8,128)(2,1)S(1)} %copy.66), kind=kLoop, calls=%fused_computation.11 | loop fusion | flops 4194304 | bytes 4194304 | tf_op jit(solution)/shard_map/concatenate | solution.py:304
  16.3 0.2 slice_reduce_fusion.1
  16.5 0.1 copy.74
  16.6 0.1 copy.64
  16.8 0.1 copy.62
  16.9 0.1 copy.63
  17.1 0.1 and_select_fusion
  17.3 0.9 iota_compare_fusion
  19.1 0.1 copy.76
  19.2 6.1 %fusion = bf16[2,16,128,512]{3,2,1,0:T(8,128)(2,1)} fusion(bf16[2,128,16,256,1]{1,3,2,0,4:T(8,128)(2,1)} %bitcast.118, pred[3,2,2,256,512]{3,4,2,1,0:T(32,128)(4,1)S(1)} %iota_compare_fusion), kind=kOutput, calls=%fused_computation.3 | convolution fusion | flops 2149580800 | bytes 6815744 | tf_op jit(solution)/shard_map/kcxa,skat->sxct/dot_general | solution.py:268
  25.3 0.6 fusion.14.active_ref
  25.9 0.1 multiply_reduce_fusion.1
  26.0 0.6 copy.82.live_ref
  26.6 0.3 copy.77
  26.9 0.2 reshape.184
  27.1 1.0 rev.7
  28.1 1.1 copy.111
  29.1 1.1 reshape.205.w1_ref
  30.2 0.3 copy.79
  30.5 0.2 reshape.186
  30.7 0.8 rev.6
  31.5 0.1 copy.112
  31.7 1.1 reshape.206.w2t_ref
  32.8 0.1 copy.113
  32.9 1.1 reshape.207.w1t_ref
  34.0 0.7 copy.86.bias_ref
  34.7 1.8 %fusion.8 = bf16[2,2,128,512]{3,2,1,0:T(8,128)(2,1)S(1)} fusion(bf16[2,128,2,256,1]{1,3,2,0,4:T(8,128)(2,1)} %bitcast.23, pred[3,2,2,256,512]{3,4,2,1,0:T(32,128)(4,1)S(1)} %copy-done.3), kind=kOutput, calls=%fused_computation.19 | convolution fusion | flops 268697600 | bytes 1310720 | tf_op jit(solution)/shard_map/kcxa,skat->sxct/dot_general | solution.py:268
  36.5 1.6 %fusion.7 = bf16[2,2,128,512]{3,2,1,0:T(8,128)(2,1)S(1)} fusion(bf16[2,128,2,256,1]{1,3,2,0,4:T(8,128)(2,1)} %bitcast.9, pred[3,2,2,256,512]{3,4,2,1,0:T(32,128)(4,1)S(1)} %copy-done.3), kind=kOutput, calls=%fused_computation.18 | convolution fusion | flops 268697600 | bytes 1310720 | tf_op jit(solution)/shard_map/kcxa,skat->sxct/dot_general | solution.py:268
  38.1 2.9 %pad_maximum_fusion.tile_ref = bf16[2,20,128,512]{3,2,1,0:T(8,128)(2,1)} fusion(bf16[2,2,128,512]{3,2,1,0:T(8,128)(2,1)S(1)} %fusion.8, bf16[2,16,128,512]{3,2,1,0:T(8,128)(2,1)S(1)} %copy-done.1, bf16[2,2,128,512]{3,2,1,0:T(8,128)(2,1)S(1)} %fusion.7), kind=kLoop, calls=%fused_computation.2 | loop fusion | flops 5242880 | bytes 10485760 | tf_op jit(solution)/shard_map/concatenate | solution.py:311
  41.1 31.4 %shard_map.129 = (bf16[2,64,4096]{2,1,0:T(8,128)(2,1)}, f32[584,384]{1,0:T(8,128)}) custom-call(s32[2]{0:T(128)} %fusion.14.active_ref, bf16[2,20,128,512]{3,2,1,0:T(8,128)(2,1)} %pad_maximum_fusion.tile_ref, f32[2,3,1,384]{3,2,1,0:T(1,128)} %copy.82.live_ref, f32[2,384]{1,0:T(2,128)} %constant.76.clone.masks_ref, ...), custom_call_target="tpu_custom_call" | custom-call | tf_op jit(solution)/shard_map/pallas_call | solution.py:183
  72.5 1.3 select_convert_fusion
  73.7 29.0 %collective-permute-start.2 = (bf16[320,384]{1,0:T(8,128)(2,1)S(1)}, bf16[320,384]{1,0:T(8,128)(2,1)S(1)}, u32[]{:S(2)}, u32[]{:S(2)}) collective-permute-start(bf16[320,384]{1,0:T(8,128)(2,1)S(1)} %select_convert_fusion), channel_id=1, source_target_pairs={{0,1},{1,0},{2,3},{3,2},{4,5},{5,4},{6,7},{7,6},{8,9},{9,8},{10,11... | collective-permute-start | bytes 737288 | tf_op jit(solution)/shard_map/ppermute | solution.py:288
  102.8 1.1 collective-permute-done.2
  104.1 5.6 %collective-permute-done.3 = bf16[160,384]{1,0:T(8,128)(2,1)S(1)} collective-permute-done((bf16[160,384]{1,0:T(8,128)(2,1)S(1)}, bf16[160,384]{1,0:T(8,128)(2,1)S(1)}, u32[]{:S(2)}, u32[]{:S(2)}) %collective-permute-start.3) | collective-permute-done | bytes 122912 | tf_op jit(solution)/shard_map/ppermute | solution.py:288
  109.8 2.3 %collective-permute-start.4 = (bf16[80,384]{1,0:T(8,128)(2,1)S(1)}, bf16[80,384]{1,0:T(8,128)(2,1)S(1)}, u32[]{:S(2)}, u32[]{:S(2)}) collective-permute-start(bf16[80,384]{1,0:T(8,128)(2,1)S(1)} %select_convert_fusion.2), channel_id=1, source_target_pairs={{0,4},{1,5},{2,6},{3,7},{4,0},{5,1},{6,2},{7,3},{8,12},{9,13},{10,... | collective-permute-start | bytes 184328 | tf_op jit(solution)/shard_map/ppermute | solution.py:288
  112.0 2.2 %collective-permute-done.4 = bf16[80,384]{1,0:T(8,128)(2,1)S(1)} collective-permute-done((bf16[80,384]{1,0:T(8,128)(2,1)S(1)}, bf16[80,384]{1,0:T(8,128)(2,1)S(1)}, u32[]{:S(2)}, u32[]{:S(2)}) %collective-permute-start.4) | collective-permute-done | bytes 61472 | tf_op jit(solution)/shard_map/ppermute | solution.py:288
  114.3 3.1 %collective-permute-start.5 = (bf16[40,384]{1,0:T(8,128)(2,1)S(1)}, bf16[40,384]{1,0:T(8,128)(2,1)S(1)}, u32[]{:S(2)}, u32[]{:S(2)}) collective-permute-start(bf16[40,384]{1,0:T(8,128)(2,1)S(1)} %select_convert_fusion.3), channel_id=1, source_target_pairs={{0,8},{1,9},{2,10},{3,11},{4,12},{5,13},{6,14},{7,15},{8,0},{9,1},... | collective-permute-start | bytes 92168 | tf_op jit(solution)/shard_map/ppermute | solution.py:288
  117.4 1.9 %collective-permute-done.5 = bf16[40,384]{1,0:T(8,128)(2,1)S(1)} collective-permute-done((bf16[40,384]{1,0:T(8,128)(2,1)S(1)}, bf16[40,384]{1,0:T(8,128)(2,1)S(1)}, u32[]{:S(2)}, u32[]{:S(2)}) %collective-permute-start.5) | collective-permute-done | bytes 30752 | tf_op jit(solution)/shard_map/ppermute | solution.py:288
  119.3 3.0 %collective-permute-start.6 = (bf16[40,384]{1,0:T(8,128)(2,1)S(1)}, bf16[40,384]{1,0:T(8,128)(2,1)S(1)}, u32[]{:S(2)}, u32[]{:S(2)}) collective-permute-start(bf16[40,384]{1,0:T(8,128)(2,1)S(1)} %add_convert_fusion), channel_id=1, source_target_pairs={{0,8},{1,9},{2,10},{3,11},{4,12},{5,13},{6,14},{7,15},{8,0},{9,1},... | collective-permute-start | bytes 92168 | tf_op jit(solution)/shard_map/ppermute | solution.py:294
  122.2 2.0 %collective-permute-done.6 = bf16[40,384]{1,0:T(8,128)(2,1)S(1)} collective-permute-done((bf16[40,384]{1,0:T(8,128)(2,1)S(1)}, bf16[40,384]{1,0:T(8,128)(2,1)S(1)}, u32[]{:S(2)}, u32[]{:S(2)}) %collective-permute-start.6) | collective-permute-done | bytes 30752 | tf_op jit(solution)/shard_map/ppermute | solution.py:294
  124.3 1.9 %collective-permute-start.7 = (bf16[80,384]{1,0:T(8,128)(2,1)S(1)}, bf16[80,384]{1,0:T(8,128)(2,1)S(1)}, u32[]{:S(2)}, u32[]{:S(2)}) collective-permute-start(bf16[80,384]{1,0:T(8,128)(2,1)S(1)} %pad_maximum_fusion.5), channel_id=1, source_target_pairs={{0,4},{1,5},{2,6},{3,7},{4,0},{5,1},{6,2},{7,3},{8,12},{9,13},{10,... | collective-permute-start | bytes 184328 | tf_op jit(solution)/shard_map/ppermute | solution.py:294
  126.1 2.4 %collective-permute-done.7 = bf16[80,384]{1,0:T(8,128)(2,1)S(1)} collective-permute-done((bf16[80,384]{1,0:T(8,128)(2,1)S(1)}, bf16[80,384]{1,0:T(8,128)(2,1)S(1)}, u32[]{:S(2)}, u32[]{:S(2)}) %collective-permute-start.7) | collective-permute-done | bytes 61472 | tf_op jit(solution)/shard_map/ppermute | solution.py:294
  128.6 1.9 %collective-permute-start.8 = (bf16[160,384]{1,0:T(8,128)(2,1)S(1)}, bf16[160,384]{1,0:T(8,128)(2,1)S(1)}, u32[]{:S(2)}, u32[]{:S(2)}) collective-permute-start(bf16[160,384]{1,0:T(8,128)(2,1)S(1)} %pad_maximum_fusion.4), channel_id=1, source_target_pairs={{0,2},{1,3},{2,0},{3,1},{4,6},{5,7},{6,4},{7,5},{8,10},{9,11},{10,... | collective-permute-start | bytes 368648 | tf_op jit(solution)/shard_map/ppermute | solution.py:294
  130.5 3.0 %collective-permute-done.8 = bf16[160,384]{1,0:T(8,128)(2,1)S(1)} collective-permute-done((bf16[160,384]{1,0:T(8,128)(2,1)S(1)}, bf16[160,384]{1,0:T(8,128)(2,1)S(1)}, u32[]{:S(2)}, u32[]{:S(2)}) %collective-permute-start.8) | collective-permute-done | bytes 122912 | tf_op jit(solution)/shard_map/ppermute | solution.py:294
  133.7 1.5 %collective-permute-done.9 = bf16[320,384]{1,0:T(8,128)(2,1)S(1)} collective-permute-done((bf16[320,384]{1,0:T(8,128)(2,1)S(1)}, bf16[320,384]{1,0:T(8,128)(2,1)S(1)}, u32[]{:S(2)}, u32[]{:S(2)}) %collective-permute-start.9) | collective-permute-done | bytes 245792 | tf_op jit(solution)/shard_map/ppermute | solution.py:294
  135.2 0.1 broadcast_select_fusion.1
  135.4 0.6 fusion.15
  136.0 0.8 multiply_reduce_fusion
  138.2 0.2 fusion.17
  138.5 0.4 reshape.190
  138.8 0.6 copy.87
  139.4 0.1 reshape.191
  139.5 1.1 copy.89
  140.6 0.4 reshape.192
  140.9 0.6 copy.88
  141.5 0.1 reshape.193
  141.6 1.1 copy.90
  142.7 0.5 fusion.16
  (62 shorter events, 2.1 us)
Async XLA Ops:
  0.6 2.1 %copy-start.4 = (bf16[2,64,4096]{2,1,0:T(8,128)(2,1)S(1)}, bf16[2,64,4096]{2,1,0:T(8,128)(2,1)}, u32[]{:S(2)}) copy-start(bf16[2,64,4096]{2,1,0:T(8,128)(2,1)} %param.11) | copy-start | bytes 3145732
  4.6 7.1 %copy-start.9 = (s32[32,3]{0,1:T(4,128)S(1)}, s32[32,3]{0,1:T(4,128)}, u32[]{:S(2)}) copy-start(s32[32,3]{0,1:T(4,128)} %param.12) | copy-start | bytes 1156
  6.6 28.1 %collective-permute-start.1 = (bf16[2,128,512]{1,2,0:T(8,128)(2,1)}, bf16[2,128,512]{1,2,0:T(8,128)(2,1)}, u32[]{:S(2)}, u32[]{:S(2)}) collective-permute-start(bf16[2,128,512]{1,2,0:T(8,128)(2,1)} %get-tuple-element.25), channel_id=1, source_target_pairs={{1,0},{2,1},{3,2},{4,3},{5,4},{6,5},{7,6},{8,7},{9,8},{10,9},{11,1... | collective-permute-start | bytes 786440 | tf_op jit(solution)/shard_map/ppermute | solution.py:306
  7.9 28.6 %collective-permute-start = (bf16[2,128,512]{1,2,0:T(8,128)(2,1)S(1)}, bf16[2,128,512]{1,2,0:T(8,128)(2,1)}, u32[]{:S(2)}, u32[]{:S(2)}) collective-permute-start(bf16[2,128,512]{1,2,0:T(8,128)(2,1)S(1)} %get-tuple-element.24), channel_id=1, source_target_pairs={{0,1},{1,2},{2,3},{3,4},{4,5},{5,6},{6,7},{7,8},{8,9},{9,10},{10,1... | collective-permute-start | bytes 786440 | tf_op jit(solution)/shard_map/ppermute | solution.py:305
  12.2 6.0 %copy-start.8 = (s32[27,3]{0,1:T(4,128)S(1)}, s32[27,3]{0,1:T(4,128)}, u32[]{:S(2)}) copy-start(s32[27,3]{0,1:T(4,128)} %constant.74.clone) | copy-start | bytes 976
  18.2 7.1 %copy-start.2 = (pred[3,2,2,256,512]{3,4,2,1,0:T(32,128)(4,1)}, pred[3,2,2,256,512]{3,4,2,1,0:T(32,128)(4,1)S(1)}, u32[]{:S(2)}) copy-start(pred[3,2,2,256,512]{3,4,2,1,0:T(32,128)(4,1)S(1)} %iota_compare_fusion) | copy-start | bytes 4718596
  19.2 6.7 %copy-start.7 = (f32[9,384]{1,0:T(8,128)S(1)}, f32[9,384]{1,0:T(8,128)}, u32[]{:S(2)}) copy-start(f32[9,384]{1,0:T(8,128)} %constant.84) | copy-start | bytes 41476
  19.2 7.4 %copy-start.5 = (bf16[64,1728]{1,0:T(8,128)(2,1)S(1)}, bf16[64,1728]{1,0:T(8,128)(2,1)}, u32[]{:S(2)}) copy-start(bf16[64,1728]{1,0:T(8,128)(2,1)} %param.13) | copy-start | bytes 663556
  27.1 3.2 %copy-start.6 = (bf16[64,1728]{1,0:T(8,128)(2,1)S(1)}, bf16[64,1728]{1,0:T(8,128)(2,1)}, u32[]{:S(2)}) copy-start(bf16[64,1728]{1,0:T(8,128)(2,1)} %param.15) | copy-start | bytes 663556
  31.6 2.4 %copy-start.10 = (f32[64]{0:T(128)S(1)}, f32[64]{0:T(128)}, u32[]{:S(2)}) copy-start(f32[64]{0:T(128)} %param.14) | copy-start | bytes 772
  32.8 1.9 %copy-start.3 = (pred[3,2,2,256,512]{3,4,2,1,0:T(32,128)(4,1)S(1)}, pred[3,2,2,256,512]{3,4,2,1,0:T(32,128)(4,1)}, u32[]{:S(2)}) copy-start(pred[3,2,2,256,512]{3,4,2,1,0:T(32,128)(4,1)} %copy-done.2) | copy-start | bytes 4718596
  34.7 3.4 %copy-start.1 = (bf16[2,16,128,512]{3,2,1,0:T(8,128)(2,1)S(1)}, bf16[2,16,128,512]{3,2,1,0:T(8,128)(2,1)}, u32[]{:S(2)}) copy-start(bf16[2,16,128,512]{3,2,1,0:T(8,128)(2,1)} %fusion) | copy-start | bytes 12582916
  72.5 31.5 %copy-start = (f32[584,384]{1,0:T(8,128)S(1)}, f32[584,384]{1,0:T(8,128)}, u32[]{:S(2)}) copy-start(f32[584,384]{1,0:T(8,128)} %get-tuple-element.7) | copy-start | bytes 2691076
  73.7 30.2 %collective-permute-start.2 = (bf16[320,384]{1,0:T(8,128)(2,1)S(1)}, bf16[320,384]{1,0:T(8,128)(2,1)S(1)}, u32[]{:S(2)}, u32[]{:S(2)}) collective-permute-start(bf16[320,384]{1,0:T(8,128)(2,1)S(1)} %select_convert_fusion), channel_id=1, source_target_pairs={{0,1},{1,0},{2,3},{3,2},{4,5},{5,4},{6,7},{7,6},{8,9},{9,8},{10,11... | collective-permute-start | bytes 737288 | tf_op jit(solution)/shard_map/ppermute | solution.py:288
  104.0 5.7 %collective-permute-start.3 = (bf16[160,384]{1,0:T(8,128)(2,1)S(1)}, bf16[160,384]{1,0:T(8,128)(2,1)S(1)}, u32[]{:S(2)}, u32[]{:S(2)}) collective-permute-start(bf16[160,384]{1,0:T(8,128)(2,1)S(1)} %select_convert_fusion.1), channel_id=1, source_target_pairs={{0,2},{1,3},{2,0},{3,1},{4,6},{5,7},{6,4},{7,5},{8,10},{9,11},{10,... | collective-permute-start | bytes 368648 | tf_op jit(solution)/shard_map/ppermute | solution.py:288
  109.8 4.5 %collective-permute-start.4 = (bf16[80,384]{1,0:T(8,128)(2,1)S(1)}, bf16[80,384]{1,0:T(8,128)(2,1)S(1)}, u32[]{:S(2)}, u32[]{:S(2)}) collective-permute-start(bf16[80,384]{1,0:T(8,128)(2,1)S(1)} %select_convert_fusion.2), channel_id=1, source_target_pairs={{0,4},{1,5},{2,6},{3,7},{4,0},{5,1},{6,2},{7,3},{8,12},{9,13},{10,... | collective-permute-start | bytes 184328 | tf_op jit(solution)/shard_map/ppermute | solution.py:288
  114.3 5.0 %collective-permute-start.5 = (bf16[40,384]{1,0:T(8,128)(2,1)S(1)}, bf16[40,384]{1,0:T(8,128)(2,1)S(1)}, u32[]{:S(2)}, u32[]{:S(2)}) collective-permute-start(bf16[40,384]{1,0:T(8,128)(2,1)S(1)} %select_convert_fusion.3), channel_id=1, source_target_pairs={{0,8},{1,9},{2,10},{3,11},{4,12},{5,13},{6,14},{7,15},{8,0},{9,1},... | collective-permute-start | bytes 92168 | tf_op jit(solution)/shard_map/ppermute | solution.py:288
  119.3 5.0 %collective-permute-start.6 = (bf16[40,384]{1,0:T(8,128)(2,1)S(1)}, bf16[40,384]{1,0:T(8,128)(2,1)S(1)}, u32[]{:S(2)}, u32[]{:S(2)}) collective-permute-start(bf16[40,384]{1,0:T(8,128)(2,1)S(1)} %add_convert_fusion), channel_id=1, source_target_pairs={{0,8},{1,9},{2,10},{3,11},{4,12},{5,13},{6,14},{7,15},{8,0},{9,1},... | collective-permute-start | bytes 92168 | tf_op jit(solution)/shard_map/ppermute | solution.py:294
  124.3 4.3 %collective-permute-start.7 = (bf16[80,384]{1,0:T(8,128)(2,1)S(1)}, bf16[80,384]{1,0:T(8,128)(2,1)S(1)}, u32[]{:S(2)}, u32[]{:S(2)}) collective-permute-start(bf16[80,384]{1,0:T(8,128)(2,1)S(1)} %pad_maximum_fusion.5), channel_id=1, source_target_pairs={{0,4},{1,5},{2,6},{3,7},{4,0},{5,1},{6,2},{7,3},{8,12},{9,13},{10,... | collective-permute-start | bytes 184328 | tf_op jit(solution)/shard_map/ppermute | solution.py:294
  128.6 4.9 %collective-permute-start.8 = (bf16[160,384]{1,0:T(8,128)(2,1)S(1)}, bf16[160,384]{1,0:T(8,128)(2,1)S(1)}, u32[]{:S(2)}, u32[]{:S(2)}) collective-permute-start(bf16[160,384]{1,0:T(8,128)(2,1)S(1)} %pad_maximum_fusion.4), channel_id=1, source_target_pairs={{0,2},{1,3},{2,0},{3,1},{4,6},{5,7},{6,4},{7,5},{8,10},{9,11},{10,... | collective-permute-start | bytes 368648 | tf_op jit(solution)/shard_map/ppermute | solution.py:294
  133.6 1.6 %collective-permute-start.9 = (bf16[320,384]{1,0:T(8,128)(2,1)S(1)}, bf16[320,384]{1,0:T(8,128)(2,1)S(1)}, u32[]{:S(2)}, u32[]{:S(2)}) collective-permute-start(bf16[320,384]{1,0:T(8,128)(2,1)S(1)} %pad_maximum_fusion.3), channel_id=1, source_target_pairs={{0,1},{1,0},{2,3},{3,2},{4,5},{5,4},{6,7},{7,6},{8,9},{9,8},{10,11... | collective-permute-start | bytes 737288 | tf_op jit(solution)/shard_map/ppermute | solution.py:294
